TPU v7x, 32 devices: a whole 2x2x4 slice. The times are simulated.
32 devices in a mesh: ctx: 16 (over z, y, x), head: 2 (over core).
Axes of the slice: x: 2, y: 2, z: 4, core: 2. Of those that a mesh axis runs over, the one named last changes fastest.
Arguments:
- hidden_in: bfloat16 [2048, 2304], P('ctx'), may hold values from -6 to 6
- out_cotangent: bfloat16 [2048, 2304], P('ctx'), may hold values from -6 to 6
- block_table: int32 [16, 2], replicated, may hold values from 0 to 31, as said below
- attend_weight: float32 [2304, 4, 4, 256], P('ctx', 'head'), may hold values from -0.1875 to 0.1875
- attend_moment: float32 [2304, 4, 4, 256], P('ctx', 'head'), may hold values from -14.934095 to 14.934095
- attend_square: float32 [2304, 4, 4, 256], P('ctx', 'head'), may hold values from 26.624 to 108.544
- output_weight: float32 [8, 256, 2304], P('head', None, 'ctx'), may hold values from -0.25 to 0.25
- output_moment: float32 [8, 256, 2304], P('head', None, 'ctx'), may hold values from -14.934095 to 14.934095
- output_square: float32 [8, 256, 2304], P('head', None, 'ctx'), may hold values from 26.624 to 108.544
- expand_weight: float32 [2304, 2, 9216], P('ctx', None, 'head'), may hold values from -0.125 to 0.125
- expand_moment: float32 [2304, 2, 9216], P('ctx', None, 'head'), may hold values from -14.934095 to 14.934095
- expand_square: float32 [2304, 2, 9216], P('ctx', None, 'head'), may hold values from 26.624 to 108.544
- shrink_weight: float32 [9216, 2304], P('head', 'ctx'), may hold values from -0.0625 to 0.0625
- shrink_moment: float32 [9216, 2304], P('head', 'ctx'), may hold values from -14.934095 to 14.934095
- shrink_square: float32 [9216, 2304], P('head', 'ctx'), may hold values from 26.624 to 108.544
- gains_weight: float32 [4, 2304], P(None, 'ctx'), may hold values from -0.8 to 0.8
- gains_moment: float32 [4, 2304], P(None, 'ctx'), may hold values from -29.86819 to 29.86819
- gains_square: float32 [4, 2304], P(None, 'ctx'), may hold values from 108.544 to 430.08
Outputs:
- hidden_out: bfloat16 [2048, 2304], P('ctx')
- hidden_grad: float32 [2048, 2304], P('ctx')
- attend_grad: float32 [2304, 4, 4, 256], P('ctx', 'head')
- attend_after: float32 [2304, 4, 4, 256], P('ctx', 'head')
- attend_mean: float32 [2304, 4, 4, 256], P('ctx', 'head')
- attend_power: float32 [2304, 4, 4, 256], P('ctx', 'head')
- output_grad: float32 [8, 256, 2304], P('head', None, 'ctx')
- output_after: float32 [8, 256, 2304], P('head', None, 'ctx')
- output_mean: float32 [8, 256, 2304], P('head', None, 'ctx')
- output_power: float32 [8, 256, 2304], P('head', None, 'ctx')
- expand_grad: float32 [2304, 2, 9216], P('ctx', None, 'head')
- expand_after: float32 [2304, 2, 9216], P('ctx', None, 'head')
- expand_mean: float32 [2304, 2, 9216], P('ctx', None, 'head')
- expand_power: float32 [2304, 2, 9216], P('ctx', None, 'head')
- shrink_grad: float32 [9216, 2304], P('head', 'ctx')
- shrink_after: float32 [9216, 2304], P('head', 'ctx')
- shrink_mean: float32 [9216, 2304], P('head', 'ctx')
- shrink_power: float32 [9216, 2304], P('head', 'ctx')
- gains_grad: float32 [4, 2304], P(None, 'ctx')
- gains_after: float32 [4, 2304], P(None, 'ctx')
- gains_mean: float32 [4, 2304], P(None, 'ctx')
- gains_power: float32 [4, 2304], P(None, 'ctx')
Inputs may be any that keep to these rules, and one draw needn't show every extreme that they name: `block_table`: row i lists the two blocks of 64 tokens held by index i of ctx, in the order in which they are laid end to end; the two numbers of a row add up to 31 and every block appears once.
All inputs are finite; a program needn't handle non-finite values.
Results may differ from a plain program's by a relative error of at most 0.02.
The roundings to bfloat16 on the way count: a program that leaves them out, or rounds other values in their place, can miss the bound.
Values may be sent and summed in bfloat16 or wider, within the bound.
No kernel may reach another device: no remote copies, remote signals or barrier semaphores. Data moves between devices by JAX's collectives and lax.ppermute only.
A program may use at most 256 MiB of HBM per device.

v0:
```python
import jax
import jax.numpy as jnp
from jax import lax
from jax.experimental import pallas as pl
from jax.experimental.pallas import tpu as pltpu
from jax.sharding import Mesh
from jax.sharding import PartitionSpec as P

STEP = 10


NORM_EPS = 1e-06
SOFT_CAP = 50.0
ROPE_BASE = 10000.0
RATE_MATRIX = 0.02
RATE_GAIN = 0.1
BETA_ONE = 0.9
BETA_TWO = 0.95
ADAM_EPS = 1e-08
DECAY = 0.1
ROWS = (((0,), (0,)), ((), ()))
LAST = (((1,), (1,)), ((), ()))
LINES = 4
F32 = jnp.float32
BF16 = jnp.bfloat16


def rope_tables(positions, head_width):
    exponent = jnp.arange(head_width // 2, dtype=F32) * (2.0 / head_width)
    frequency = ROPE_BASE ** (-exponent)
    angle = positions.astype(F32)[:, None] * frequency[None, :]
    return (jnp.cos(angle), jnp.sin(angle))


def rotate(values, cosine, sine_table):
    middle = values.shape[-1] // 2
    front_half = values[..., :middle]
    back_half = values[..., middle:]
    return jnp.concatenate(
        [
            front_half * cosine - back_half * sine_table,
            back_half * cosine + front_half * sine_table,
        ],
        axis=-1,
    )


def norm_factor(values):
    return lax.rsqrt(jnp.mean(values * values, axis=-1, keepdims=True) + NORM_EPS)


def norm_apply(values, norm_gain):
    return values * norm_factor(values) * (1.0 + norm_gain)


def norm_back(values, norm_gain, grad_out):
    factor = norm_factor(values)
    weighted = grad_out * (1.0 + norm_gain)
    grad_in = factor * weighted - values * factor * factor * factor * jnp.mean(
        values * weighted, axis=-1, keepdims=True
    )
    grad_gain = jnp.sum(grad_out * values * factor, axis=0)
    return (grad_in, grad_gain)


def adam_step(weight, moment, square, grad, rate, decay):
    moment_new = BETA_ONE * moment + (1.0 - BETA_ONE) * grad
    square_new = BETA_TWO * square + (1.0 - BETA_TWO) * grad * grad
    mean_hat = moment_new / (1.0 - BETA_ONE**STEP)
    power_hat = square_new / (1.0 - BETA_TWO**STEP)
    updated = weight - rate * (mean_hat / (jnp.sqrt(power_hat) + ADAM_EPS) + decay * weight)
    return (updated, moment_new, square_new)


def pick(array, index):
    return lax.dynamic_index_in_dim(array, index, 0, keepdims=False)


def put(array, part, index, dim=0):
    return lax.dynamic_update_slice_in_dim(array, jnp.expand_dims(part, dim), index, dim)


def mirror(number, bits):
    return sum(((number >> i) & 1) << (bits - 1 - i) for i in range(bits))


def after(value, *events):
    return lax.optimization_barrier((value,) + events)[0]


class Grid:
    def __init__(self):
        self.plane = lax.axis_size("place")
        self.bits = self.plane.bit_length() - 1
        self.line = lax.axis_index("line")
        self.place = lax.axis_index("place")
        self.core = lax.axis_index("head")

    def along(self, value, step):
        pairs = [(i, i ^ step) for i in range(LINES)]
        return lax.ppermute(value, "line", pairs)

    def across(self, value):
        return lax.ppermute(value, "head", [(0, 1), (1, 0)])

    def within(self, value, phase):
        pairs = []
        for i in range(self.plane):
            for core in range(2):
                bit = phase if core == 0 else self.bits - 1 - phase
                pairs.append((2 * i + core, 2 * (i ^ (1 << bit)) + core))
        return lax.ppermute(value, ("place", "head"), pairs)

    def place_of(self, mask):
        return self.place ^ jnp.where(self.core == 0, mask, mirror(mask, self.bits))

    def token_gather(self, value, *events):
        near = self.along(value, 1)
        far = self.along(value, 3)
        middle = self.along(far, 1)
        own = jnp.zeros((LINES,) + value.shape, value.dtype)
        for step, part in enumerate((value, near, middle, far)):
            own = put(own, part, self.line ^ step)
        own = own.reshape(-1, value.shape[-1])
        if events:
            own = after(own, *events)
        return jnp.concatenate([own, self.across(own)], axis=0)

    def token_reduce(self, own, other, *events):
        if events:
            other = after(other, *events)
        mine = (own + self.across(other).astype(F32)).reshape(LINES, -1, own.shape[-1])
        block = [pick(mine, self.line ^ step) for step in range(LINES)]
        passed = self.along(block[2].astype(BF16), 1)
        near = self.along(block[1].astype(BF16), 1)
        far = self.along((block[3] + passed.astype(F32)).astype(BF16), 3)
        return block[0] + near.astype(F32) + far.astype(F32)

    def line_swap(self, blocks):
        return lax.all_to_all(blocks, "line", split_axis=0, concat_axis=0, tiled=True)

    def plane_gather(self, own, *events):
        parts = {0: own}
        for phase in range(self.bits):
            for mask in range(1 << phase):
                given = parts[mask]
                if mask and events:
                    given = after(given, *events)
                parts[mask | (1 << phase)] = self.within(given, phase)
        return parts

    def plane_reduce(self, parts, *events):
        parts = dict(parts)
        for phase in reversed(range(self.bits)):
            for mask in reversed(range(1 << phase)):
                given = parts[mask | (1 << phase)]
                if phase == 0 and events:
                    given = after(given, *events)
                got = self.within(given, phase)
                parts[mask] = parts[mask] + got.astype(F32)
                if mask or phase:
                    parts[mask] = parts[mask].astype(BF16)
        return parts[0]

    def spread(self, own, *events):
        return self.assemble(self.plane_gather(own, *events))

    def assemble(self, parts):
        full = jnp.zeros((LINES, self.plane) + parts[0].shape[1:], parts[0].dtype)
        for mask, part in parts.items():
            full = put(full, part, self.place_of(mask), 1)
        return full.reshape(-1, parts[0].shape[-1])

    def bulk_spread(self, own):
        full = lax.all_gather(own, "place", axis=1, tiled=True)
        return full.reshape(-1, own.shape[-1])

    def bulk_sum(self, terms):
        shaped = terms.reshape(LINES, -1, terms.shape[-1])
        return lax.psum_scatter(shaped, "place", scatter_dimension=1, tiled=True)

    def all_terms(self, terms, *events):
        shaped = terms.reshape(LINES, self.plane, -1, terms.shape[-1])
        parts = {
            mask: lax.dynamic_index_in_dim(shaped, self.place_of(mask), 1, keepdims=False)
            for mask in range(self.plane)
        }
        return self.plane_reduce(parts, *events).astype(BF16)

    def first_half(self, values):
        half = values.shape[0] // 2
        swapped = jnp.concatenate([values[half:], values[:half]])
        return jnp.where(self.core == 0, values, swapped)


TILE = 128


def rows_per_step(local_width):
    return 16 if local_width % 16 == 0 else local_width


def attend_rows(array):
    rows, groups, slots, width = array.shape
    tiles = width // TILE
    shaped = array.reshape(rows, groups, slots, tiles, TILE).transpose(0, 1, 3, 2, 4)
    return shaped.reshape(-1, TILE)


def attend_from_rows(array, shape):
    rows, groups, slots, width = shape
    tiles = width // TILE
    shaped = array.reshape(rows, groups, tiles, slots, TILE).transpose(0, 1, 3, 2, 4)
    return shaped.reshape(shape)


def row_block(rows, height):
    return pl.BlockSpec((rows * height, TILE), lambda i, *_: (i, 0))


def pack_expand(weight):
    local_width, _, width = weight.shape
    rows = rows_per_step(local_width)
    quarter = width // LINES

    def kernel(in_ref, *out_refs):
        for gate, out_ref in enumerate(out_refs):
            for line in range(LINES):
                part = in_ref[:, gate, line * quarter : (line + 1) * quarter]
                out_ref[line] = part.astype(BF16)

    pack = jax.ShapeDtypeStruct((LINES, local_width, quarter), BF16)
    return pl.pallas_call(
        kernel,
        out_shape=[pack] * 2,
        grid=(local_width // rows,),
        in_specs=[pl.BlockSpec((rows, 2, width), lambda i: (i, 0, 0))],
        out_specs=[pl.BlockSpec((LINES, rows, quarter), lambda i: (0, i, 0))] * 2,
        compiler_params=pltpu.CompilerParams(vmem_limit_bytes=32 << 20),
        cost_estimate=pl.CostEstimate(flops=0, bytes_accessed=6 * weight.size, transcendentals=0),
        name="pack_expand",
    )(weight)


def pack_shrink(weight):
    width, local_width = weight.shape
    rows = rows_per_step(local_width)
    quarter = width // LINES

    def kernel(in_ref, out_ref):
        for line in range(LINES):
            out_ref[line] = in_ref[:, line * quarter : (line + 1) * quarter].astype(BF16)

    return pl.pallas_call(
        kernel,
        out_shape=jax.ShapeDtypeStruct((LINES, local_width, quarter), BF16),
        grid=(local_width // rows,),
        in_specs=[pl.BlockSpec((rows, width), lambda i: (i, 0))],
        out_specs=pl.BlockSpec((LINES, rows, quarter), lambda i: (0, i, 0)),
        compiler_params=pltpu.CompilerParams(vmem_limit_bytes=32 << 20),
        cost_estimate=pl.CostEstimate(flops=0, bytes_accessed=6 * weight.size, transcendentals=0),
        name="pack_shrink",
    )(weight.T)


def pack_attend(weight, gains, core):
    local_width, groups, slots, width = weight.shape
    rows = rows_per_step(local_width)
    tiles = width // TILE
    height = groups * slots * tiles
    columns = 2 * width + TILE

    def kernel(core_ref, in_ref, gains_ref, own_ref, other_ref):
        for out_ref, member in ((own_ref, core_ref[0]), (other_ref, 1 - core_ref[0])):
            for group in range(groups):
                for pair in range(2):
                    for tile in range(tiles):
                        first = (group * tiles + tile) * slots + 2 * pair
                        chosen = pl.ds(first + member, rows, stride=height)
                        column = (pair * tiles + tile) * TILE
                        out_ref[group, :, column : column + TILE] = in_ref[chosen, :].astype(BF16)
                out_ref[group, :, 2 * width :] = gains_ref[...].astype(BF16)

    pack = jax.ShapeDtypeStruct((groups, local_width, columns), BF16)
    gain_columns = jnp.pad(gains.T, ((0, 0), (0, TILE - gains.shape[0])))
    return pl.pallas_call(
        kernel,
        out_shape=[pack] * 2,
        grid_spec=pltpu.PrefetchScalarGridSpec(
            num_scalar_prefetch=1,
            grid=(local_width // rows,),
            in_specs=[
                row_block(rows, height),
                pl.BlockSpec((rows, TILE), lambda i, *_: (i, 0)),
            ],
            out_specs=[pl.BlockSpec((groups, rows, columns), lambda i, *_: (0, i, 0))] * 2,
        ),
        compiler_params=pltpu.CompilerParams(vmem_limit_bytes=32 << 20),
        cost_estimate=pl.CostEstimate(flops=0, bytes_accessed=6 * weight.size, transcendentals=0),
        name="pack_attend",
    )(core.reshape(1), attend_rows(weight), gain_columns)


def adam_tile(grad, chosen, in_refs, out_refs):
    weight, moment, square = (ref[chosen] for ref in in_refs)
    updated = adam_step(weight, moment, square, grad, RATE_MATRIX, DECAY)
    for ref, value in zip(out_refs, (grad,) + updated, strict=True):
        ref[chosen] = value


def adam_call(kernel, scalars, grads, grad_specs, states, state_spec, steps, name, weight):
    return pl.pallas_call(
        kernel,
        out_shape=[jax.ShapeDtypeStruct(states[0].shape, F32)] * 4,
        grid_spec=pltpu.PrefetchScalarGridSpec(
            num_scalar_prefetch=len(scalars),
            grid=(steps,),
            in_specs=grad_specs + [state_spec] * 3,
            out_specs=[state_spec] * 4,
        ),
        compiler_params=pltpu.CompilerParams(vmem_limit_bytes=40 << 20),
        cost_estimate=waiting(weight),
        name=name,
    )(*scalars, *grads, *states)


def adam_expand(weight, moment, square, grad):
    local_width, _, width = weight.shape
    rows = rows_per_step(local_width)
    quarter = width // LINES

    def kernel(grad_ref, *refs):
        for gate in range(2):
            for line in range(LINES):
                chosen = (slice(None), gate, slice(line * quarter, (line + 1) * quarter))
                grad = grad_ref[line, :, gate * quarter : (gate + 1) * quarter]
                adam_tile(grad.astype(F32), chosen, refs[:3], refs[3:])

    return adam_call(
        kernel,
        (),
        [grad],
        [pl.BlockSpec((LINES, rows, 2 * quarter), lambda i: (0, i, 0))],
        [weight, moment, square],
        pl.BlockSpec((rows, 2, width), lambda i: (i, 0, 0)),
        local_width // rows,
        "adam_expand",
        60,
    )


def adam_attend(weight, moment, square, own, other, core):
    shape = weight.shape
    local_width, groups, slots, width = shape
    rows = rows_per_step(local_width)
    tiles = width // TILE
    height = groups * slots * tiles

    def kernel(core_ref, own_ref, other_ref, *refs):
        in_refs, out_refs = refs[:3], refs[3:]
        for grad_ref, member in ((own_ref, core_ref[0]), (other_ref, 1 - core_ref[0])):
            for group in range(groups):
                for pair in range(2):
                    for tile in range(tiles):
                        first = (group * tiles + tile) * slots + 2 * pair
                        chosen = (pl.ds(first + member, rows, stride=height), slice(None))
                        column = (pair * tiles + tile) * TILE
                        grad = grad_ref[group, :, column : column + TILE].astype(F32)
                        adam_tile(grad, chosen, in_refs, out_refs)

    results = adam_call(
        kernel,
        (core.reshape(1),),
        [own, other],
        [pl.BlockSpec((groups, rows, own.shape[-1]), lambda i, *_: (0, i, 0))] * 2,
        [attend_rows(a) for a in (weight, moment, square)],
        row_block(rows, height),
        local_width // rows,
        "adam_attend",
        10,
    )
    return [attend_from_rows(a, shape) for a in results]


def adam_shrink(weight, moment, square, grad):
    width, local_width = weight.shape
    rows = rows_per_step(local_width)
    quarter = width // LINES

    def kernel(grad_ref, *refs):
        for line in range(LINES):
            chosen = (slice(None), slice(line * quarter, (line + 1) * quarter))
            adam_tile(grad_ref[line].astype(F32), chosen, refs[:3], refs[3:])

    results = adam_call(
        kernel,
        (),
        [grad],
        [pl.BlockSpec((LINES, rows, quarter), lambda i: (0, i, 0))],
        [a.T for a in (weight, moment, square)],
        pl.BlockSpec((rows, width), lambda i: (i, 0)),
        local_width // rows,
        "adam_shrink",
        40,
    )
    return [a.T for a in results]


LINE_WEIGHT = 60
OWN_WEIGHT = 3


def waiting(microseconds):
    return pl.CostEstimate(
        flops=int(microseconds * 1e-6 * PEAK), bytes_accessed=0, transcendentals=0
    )


def plain_norm(values):
    tokens, width = values.shape
    rows = tokens // 2

    def kernel(in_ref, out_ref):
        wide = in_ref[...].astype(F32)
        out_ref[...] = wide * norm_factor(wide)

    block = pl.BlockSpec((rows, width), lambda j: (j, 0))
    return pl.pallas_call(
        kernel,
        out_shape=jax.ShapeDtypeStruct((tokens, width), F32),
        grid=(2,),
        in_specs=[block],
        out_specs=block,
        compiler_params=pltpu.CompilerParams(vmem_limit_bytes=24 << 20),
        cost_estimate=waiting(LINE_WEIGHT),
        name="plain_norm",
    )(values)


def last_grad(values, gain, grad_out, carried):
    def kernel(value_ref, gain_ref, grad_ref, carried_ref, out_ref):
        wide = value_ref[...].astype(F32)
        factor = norm_factor(wide)
        weighted = grad_ref[...] * (1.0 + gain_ref[...])
        mean = jnp.mean(wide * weighted, axis=-1, keepdims=True)
        out_ref[...] = carried_ref[...] + (
            factor * weighted - wide * factor * factor * factor * mean
        )

    return pl.pallas_call(
        kernel,
        out_shape=jax.ShapeDtypeStruct(values.shape, F32),
        compiler_params=pltpu.CompilerParams(vmem_limit_bytes=24 << 20),
        cost_estimate=waiting(OWN_WEIGHT),
        name="last_grad",
    )(values, gain[None], grad_out, carried)


PEAK = 1.15e15
ATTEND_WEIGHT = 30
ATTEND_BACK_WEIGHT = 100


def query_rows(tokens, keys):
    rows = tokens
    while rows > 64 and rows * keys > 1 << 19:
        rows //= 2
    return rows


def scores(queries, keys, query_spots, key_spots):
    raw = dot_last(queries, keys)
    bent = jnp.tanh(raw * (queries.shape[-1] ** (-0.5) / SOFT_CAP))
    return bent, jnp.where(key_spots <= query_spots, jnp.exp(SOFT_CAP * bent), 0.0)


def attend_forward(queries, keys, values, query_spots, key_spots):
    tokens, width = queries.shape
    count = keys.shape[0]
    rows = query_rows(tokens, count)

    def kernel(q_ref, k_ref, v_ref, spot_ref, key_spot_ref, total_ref, summed_ref, mixed_ref):
        _, weight = scores(q_ref[...], k_ref[...], spot_ref[...], key_spot_ref[...])
        total = jnp.sum(weight, axis=-1, keepdims=True)
        summed = jnp.dot(weight.astype(BF16), v_ref[...], preferred_element_type=F32)
        total_ref[...] = total
        summed_ref[...] = summed
        mixed_ref[...] = (summed / total).astype(BF16)

    def block(size):
        return pl.BlockSpec((rows, size), lambda j: (j, 0))

    return pl.pallas_call(
        kernel,
        out_shape=[
            jax.ShapeDtypeStruct((tokens, 1), F32),
            jax.ShapeDtypeStruct((tokens, width), F32),
            jax.ShapeDtypeStruct((tokens, width), BF16),
        ],
        grid=(tokens // rows,),
        in_specs=[block(width)] + [whole((count, width))] * 2 + [block(1), whole((1, count))],
        out_specs=[block(1), block(width), block(width)],
        compiler_params=pltpu.CompilerParams(vmem_limit_bytes=40 << 20),
        cost_estimate=pl.CostEstimate(
            flops=int(ATTEND_WEIGHT * 1e-6 * PEAK), bytes_accessed=0, transcendentals=0
        ),
        name="attend_forward",
    )(queries, keys, values, query_spots[:, None], key_spots[None, :])


def attend_backward(queries, keys, values, query_spots, key_spots, total, summed, grad_mixed, core):
    tokens, width = queries.shape
    count = keys.shape[0]
    rows = query_rows(tokens, count)

    def kernel(
        core_ref, q_ref, k_ref, v_ref, spot_ref, key_spot_ref, total_ref, summed_ref, grad_ref,
        query_out, kept_ref, given_ref, key_sums, value_sums,
    ):
        queries, keys = q_ref[...], k_ref[...]
        bent, weight = scores(queries, keys, spot_ref[...], key_spot_ref[...])
        total, grad_mixed = total_ref[...], grad_ref[...]
        grad_summed = (grad_mixed / total).astype(BF16)
        delta = jnp.sum(grad_mixed * summed_ref[...], axis=-1, keepdims=True) / (total * total)
        grad_weight = dot_last(grad_summed, v_ref[...]) - delta
        scale = width ** (-0.5)
        grad_raw = (weight * grad_weight * (1.0 - bent * bent) * scale).astype(BF16)
        query_out[...] = jnp.dot(grad_raw, keys, preferred_element_type=F32)
        grad_keys = dot_rows(grad_raw, queries)
        grad_values = dot_rows(weight.astype(BF16), grad_summed)
        turn = pl.program_id(0)

        @pl.when(turn == 0)
        def _():
            key_sums[...] = grad_keys
            value_sums[...] = grad_values

        @pl.when(turn > 0)
        def _():
            key_sums[...] += grad_keys
            value_sums[...] += grad_values

        @pl.when(turn == pl.num_programs(0) - 1)
        def _():
            has_keys = core_ref[0] == 0
            kept_ref[...] = jnp.where(has_keys, key_sums[...], value_sums[...])
            given_ref[...] = jnp.where(has_keys, value_sums[...], key_sums[...]).astype(BF16)

    def block(size):
        return pl.BlockSpec((rows, size), lambda j, *_: (j, 0))

    def all_of(shape):
        return pl.BlockSpec(shape, lambda j, *_: (0, 0), pipeline_mode=pl.Buffered(1))

    return pl.pallas_call(
        kernel,
        out_shape=[
            jax.ShapeDtypeStruct((tokens, width), F32),
            jax.ShapeDtypeStruct((count, width), F32),
            jax.ShapeDtypeStruct((count, width), BF16),
        ],
        grid_spec=pltpu.PrefetchScalarGridSpec(
            num_scalar_prefetch=1,
            grid=(tokens // rows,),
            in_specs=[block(width)]
            + [all_of((count, width))] * 2
            + [block(1), all_of((1, count)), block(1), block(width), block(width)],
            out_specs=[block(width)] + [all_of((count, width))] * 2,
            scratch_shapes=[pltpu.VMEM((count, width), F32)] * 2,
        ),
        compiler_params=pltpu.CompilerParams(vmem_limit_bytes=56 << 20),
        cost_estimate=pl.CostEstimate(
            flops=int(ATTEND_BACK_WEIGHT * 1e-6 * PEAK), bytes_accessed=0, transcendentals=0
        ),
        name="attend_backward",
    )(
        core.reshape(1), queries, keys, values, query_spots[:, None], key_spots[None, :],
        total, summed, grad_mixed,
    )


GELU_SCALE = 0.7978845608028654
GELU_CUBE = 0.044715


def dot_last(left, right):
    return lax.dot_general(left, right, LAST, preferred_element_type=F32)


def dot_rows(left, right):
    return lax.dot_general(left, right, ROWS, preferred_element_type=F32)


def hidden_step(units):
    return 384 if units % 384 == 0 else units


def whole(shape):
    return pl.BlockSpec(shape, lambda j: (0,) * len(shape), pipeline_mode=pl.Buffered(1))


def columns(rows, step, first=0):
    return pl.BlockSpec((rows, step), lambda j: (0, first + j))


def gate_and_up(normed, gate_weight, up_shrink):
    tokens, width = normed.shape
    units = gate_weight.shape[1]
    step = hidden_step(units)

    def kernel(x_ref, gate_w, up_w, gate_ref, up_ref, inner_ref):
        weights = jnp.concatenate([gate_w[...], up_w[...]], axis=1)
        both = jnp.dot(x_ref[...], weights, preferred_element_type=F32)
        gate, up = both[:, :step], both[:, step:]
        gate_ref[...] = gate
        up_ref[...] = up
        bend = jnp.tanh(GELU_SCALE * (gate + GELU_CUBE * gate * gate * gate))
        inner_ref[...] = (0.5 * gate * (1.0 + bend) * up).astype(BF16)

    size = tokens * units
    return pl.pallas_call(
        kernel,
        out_shape=[jax.ShapeDtypeStruct((tokens, units), kind) for kind in (F32, F32, BF16)],
        grid=(units // step,),
        in_specs=[whole((tokens, width)), columns(width, step), columns(width, step)],
        out_specs=[columns(tokens, step)] * 3,
        compiler_params=pltpu.CompilerParams(vmem_limit_bytes=32 << 20),
        cost_estimate=pl.CostEstimate(
            flops=4 * size * width, bytes_accessed=4 * units * width, transcendentals=size
        ),
        name="gate_and_up",
    )(normed, gate_weight, up_shrink)


def gate_and_up_back(grad_feed, gate, up, up_shrink):
    tokens, width = grad_feed.shape
    units = gate.shape[1]
    step = hidden_step(units)

    def kernel(feed_ref, gate_ref, up_ref, shrink_w, out_ref):
        grad_inner = jnp.dot(feed_ref[...], shrink_w[...], preferred_element_type=F32)
        gate, up = gate_ref[...], up_ref[...]
        square = gate * gate
        bend = jnp.tanh(GELU_SCALE * (gate + GELU_CUBE * gate * square))
        slope = 0.5 * (1.0 + bend) + 0.5 * gate * (1.0 - bend * bend) * (
            GELU_SCALE * (1.0 + 3.0 * GELU_CUBE * square)
        )
        first = pl.multiple_of(pl.program_id(0) * step, TILE)
        out_ref[:, pl.ds(first, step)] = (grad_inner * up * slope).astype(BF16)
        out_ref[:, pl.ds(units + first, step)] = (
            grad_inner * (0.5 * gate * (1.0 + bend))
        ).astype(BF16)

    size = tokens * units
    return pl.pallas_call(
        kernel,
        out_shape=jax.ShapeDtypeStruct((tokens, 2 * units), BF16),
        grid=(units // step,),
        in_specs=[whole((tokens, width))]
        + [columns(tokens, step)] * 2
        + [columns(width, step, units // step)],
        out_specs=pl.BlockSpec((tokens, 2 * units), lambda j: (0, 0)),
        compiler_params=pltpu.CompilerParams(vmem_limit_bytes=32 << 20),
        cost_estimate=pl.CostEstimate(
            flops=2 * size * width, bytes_accessed=2 * units * width, transcendentals=size
        ),
        name="gate_and_up_back",
    )(grad_feed, gate, up, up_shrink)


def body(
    hidden_in,
    out_cotangent,
    block_table,
    attend_weight,
    attend_moment,
    attend_square,
    output_weight,
    output_moment,
    output_square,
    expand_weight,
    expand_moment,
    expand_square,
    shrink_weight,
    shrink_moment,
    shrink_square,
    gains_weight,
    gains_moment,
    gains_square,
):
    grid = Grid()
    core = grid.core
    half_rows = hidden_in.shape[0] // 2
    local_width, group_count, slot_count, head_width = attend_weight.shape

    line_table = block_table.reshape(LINES, grid.plane, 2).transpose(1, 2, 0)
    offsets = jnp.arange(half_rows, dtype=jnp.int32)
    all_spots = (line_table[..., None] * half_rows + offsets).reshape(grid.plane, -1)
    own_spots = grid.first_half(pick(all_spots, grid.place))
    key_spots = all_spots.reshape(-1)
    line_rows = own_spots.shape[0]
    half = line_rows // 2

    own_in = lax.dynamic_slice_in_dim(hidden_in, core * half_rows, half_rows)
    own_out = lax.dynamic_slice_in_dim(out_cotangent, core * half_rows, half_rows)
    line_in = lax.all_gather(own_in, "line", axis=0, tiled=True)
    all_in = jnp.concatenate([line_in, grid.across(line_in)], axis=0)

    def by_group(own, other):
        got = grid.across(other)
        return jnp.where(core == 0, jnp.concatenate([own, got]), jnp.concatenate([got, own]))

    def group_return(blocks):
        halves = blocks.reshape((2, group_count) + blocks.shape[1:])
        return pick(halves, core), grid.across(pick(halves, 1 - core))

    attend_columns = 2 * head_width + TILE
    output_pack = (
        output_weight.astype(BF16)
        .reshape(group_count, 2, head_width, local_width)
        .transpose(1, 0, 3, 2)
    )
    packs = pack_attend(attend_weight, gains_weight, core)
    packs = [
        jnp.concatenate([pack, pick(output_pack, member)], axis=2)
        for pack, member in zip(packs, (core, 1 - core), strict=True)
    ]
    joined_rows_here = grid.line_swap(by_group(*packs))
    attend_rows_here = joined_rows_here[..., :attend_columns]
    output_rows_here = joined_rows_here[..., attend_columns:]
    gate_pack, up_pack = pack_expand(expand_weight)
    attend_and_gains = grid.spread(attend_rows_here)
    attend_full = attend_and_gains[:, : 2 * head_width]
    gain_count = gains_weight.shape[0]
    gains_all = attend_and_gains[:, 2 * head_width :][:, :gain_count].T.astype(F32)

    gate_rows_here = grid.line_swap(after(gate_pack, joined_rows_here))
    units = gate_rows_here.shape[2]
    gate_full = grid.bulk_spread(gate_rows_here)
    shrink_pack = pack_shrink(after(shrink_weight, attend_rows_here))
    up_shrink_pack = jnp.concatenate([up_pack, shrink_pack], axis=2)

    normed_plain = plain_norm(all_in)
    normed_line = (normed_plain * (1.0 + gains_all[0])).astype(BF16)
    projected = jnp.dot(
        after(normed_line, gate_rows_here), attend_full, preferred_element_type=F32
    )
    up_shrink_rows_here = grid.line_swap(after(up_shrink_pack, gate_rows_here))
    up_shrink_full = grid.bulk_spread(up_shrink_rows_here)
    cosine, sine_table = rope_tables(own_spots, head_width)
    pair_pre = projected[:, head_width:]
    pair_b = jnp.where(core == 0, rotate(pair_pre, cosine, sine_table), pair_pre).astype(BF16)
    pair_parts = grid.plane_gather(grid.first_half(pair_b))
    queries_b = rotate(projected[:, :head_width], cosine, sine_table).astype(BF16)
    pair_all = jnp.zeros((grid.plane,) + pair_b.shape, BF16)
    for mask, part in pair_parts.items():
        pair_all = put(pair_all, part, grid.place_of(mask))
    pair_all = pair_all.reshape(-1, head_width)
    pair_other = grid.across(pair_all)

    output_full = grid.spread(after(output_rows_here, pair_parts[3]))

    keys_b = jnp.where(core == 0, pair_all, pair_other)
    values_b = jnp.where(core == 0, pair_other, pair_all)
    row_total, summed, mixed_b = attend_forward(queries_b, keys_b, values_b, own_spots, key_spots)

    def halves_last(*pairs):
        other = sum(dot_last(left[half:], right) for left, right in pairs).astype(BF16)
        own = sum(dot_last(after(left[:half], other), right) for left, right in pairs)
        return own, other

    attend_sum = grid.token_reduce(*halves_last((after(mixed_b, up_shrink_rows_here), output_full)))

    hidden = own_in.astype(F32)
    first_sum = hidden + norm_apply(attend_sum, gains_all[1])
    normed_two_b = norm_apply(first_sum, gains_all[2]).astype(BF16)
    normed_two_line = grid.token_gather(normed_two_b, gate_full)
    gate_act, up_act, inner_b = gate_and_up(normed_two_line, gate_full, up_shrink_full)
    up_full, shrink_full = up_shrink_full[:, :units], up_shrink_full[:, units:]
    feed_sum = grid.token_reduce(*halves_last((inner_b, shrink_full)))
    own_hidden_out = (first_sum + norm_apply(feed_sum, gains_all[3])).astype(BF16)

    grad_out = own_out.astype(F32)
    grad_feed, gain_four = norm_back(feed_sum, gains_all[3], grad_out)
    grad_feed_line = grid.token_gather(grad_feed.astype(BF16))
    grad_both_b = gate_and_up_back(grad_feed_line, gate_act, up_act, up_shrink_full)
    expand_terms = dot_rows(normed_two_line, grad_both_b).astype(BF16)
    expand_sums = grid.bulk_sum(expand_terms)
    grad_both_b = after(grad_both_b, expand_terms)
    grad_two_parts = halves_last(
        (grad_both_b[:, :units], gate_full), (grad_both_b[:, units:], up_full)
    )
    grad_two = grid.token_reduce(*grad_two_parts)
    shrink_terms = dot_rows(grad_feed_line, after(inner_b, grad_two)).astype(BF16)
    shrink_sums = grid.bulk_sum(shrink_terms)

    grad_first_norm, gain_three = norm_back(first_sum, gains_all[2], grad_two)
    grad_first = grad_out + grad_first_norm
    grad_attend, gain_two = norm_back(attend_sum, gains_all[1], grad_first)
    grad_attend_line = grid.token_gather(grad_attend.astype(BF16))
    grad_mixed = jnp.dot(grad_attend_line, output_full, preferred_element_type=F32)
    grad_query, kept, given = attend_backward(
        queries_b, keys_b, values_b, own_spots, key_spots, row_total, summed, grad_mixed, core
    )
    pair_terms = kept + grid.across(given).astype(F32)
    pair_terms = pair_terms.astype(BF16).reshape(grid.plane, line_rows, head_width)
    pair_grad = grid.plane_reduce(
        {m: pick(pair_terms, grid.place_of(m)) for m in range(grid.plane)}
    )
    pair_grad = grid.first_half(pair_grad)
    output_terms = dot_rows(grad_attend_line, mixed_b).astype(BF16)
    grad_query_pre = rotate(grad_query, cosine, -sine_table)
    grad_pair_pre = jnp.where(core == 0, rotate(pair_grad, cosine, -sine_table), pair_grad)
    grad_proj_b = jnp.concatenate([grad_query_pre, grad_pair_pre], axis=1).astype(BF16)
    own_part, other_part = halves_last((grad_proj_b, attend_full))
    gain_one = jnp.sum(own_part * normed_plain[:half], axis=0) + jnp.sum(
        other_part.astype(F32) * normed_plain[half:], axis=0
    )
    grad_normed = grid.token_reduce(own_part, other_part)
    own_hidden_grad = last_grad(own_in, gains_all[0], grad_normed, grad_first)
    expand_back = grid.line_swap(expand_sums)

    gain_terms = jnp.stack([gain_one, gain_two, gain_three, gain_four], axis=1)
    gain_terms = jnp.pad(gain_terms, ((0, 0), (2 * head_width, TILE - gain_count)))
    attend_terms = dot_rows(normed_line, jnp.pad(grad_proj_b, ((0, 0), (0, TILE)))) + gain_terms
    joined_terms = jnp.concatenate([attend_terms.astype(BF16), output_terms], axis=1)
    joined_sums = grid.bulk_sum(joined_terms)
    shrink_back = grid.line_swap(after(shrink_sums, expand_back))
    joined = grid.line_swap(after(joined_sums, shrink_back))
    attend_line = joined[..., :attend_columns]
    output_back = group_return(joined[..., attend_columns:])
    attend_back = group_return(attend_line)
    gain_parts = attend_line[:, :, 2 * head_width : 2 * head_width + gain_count]
    gains_grad = jnp.sum(gain_parts.astype(F32), axis=0).T
    gains_grad = gains_grad + grid.across(gains_grad)

    def both_halves(value):
        other = grid.across(value)
        return jnp.where(
            core == 0, jnp.concatenate([value, other]), jnp.concatenate([other, value])
        )

    hidden_out = both_halves(own_hidden_out)
    hidden_grad = both_halves(own_hidden_grad)

    shrink_new = adam_shrink(shrink_weight, shrink_moment, shrink_square, shrink_back)
    expand_new = adam_expand(expand_weight, expand_moment, expand_square, expand_back)
    attend_new = adam_attend(
        attend_weight, attend_moment, attend_square, attend_back[0], attend_back[1], core
    )
    output_heads = jnp.where(core == 0, jnp.stack(output_back), jnp.stack(output_back[::-1]))
    output_grad = output_heads.transpose(1, 0, 3, 2).reshape(output_weight.shape).astype(F32)
    output_new = adam_step(
        output_weight, output_moment, output_square, output_grad, RATE_MATRIX, DECAY
    )
    gains_new = adam_step(
        gains_weight, gains_moment, gains_square, gains_grad, RATE_GAIN, 0.0
    )
    return (
        hidden_out,
        hidden_grad,
        *attend_new,
        output_grad,
        *output_new,
        *expand_new,
        *shrink_new,
        gains_grad,
        *gains_new,
    )


def solution(mesh):
    count, cores = mesh.shape["ctx"], mesh.shape["head"]
    devices = mesh.devices.reshape(LINES, count // LINES, cores)
    fine = Mesh(devices, ("line", "place", "head"))
    ctx = ("line", "place")
    tokens = P(ctx, None)
    attend = P(ctx, "head", None, None)
    output = P("head", None, ctx)
    expand = P(ctx, None, "head")
    shrink = P("head", ctx)
    gains = P(None, ctx)
    in_specs = (tokens, tokens, P()) + sum(
        ((spec,) * 3 for spec in (attend, output, expand, shrink, gains)), ()
    )
    out_specs = (tokens, tokens) + sum(
        ((spec,) * 4 for spec in (attend, output, expand, shrink, gains)), ()
    )
    return jax.shard_map(body, mesh=fine, in_specs=in_specs, out_specs=out_specs, check_vma=False)
```

profile of v0, /device:TPU:0, one launch (start us, length us, event | category | flops | bytes accessed | tf_op | source)
XLA Modules:
  0.0 656.7 jit_solution(16640093791188591052)
XLA Ops:
  14.1 6.2 all-to-all-start
  23.6 6.2 pack_expand.1
  31.4 29.1 %all-to-all-done = bf16[4,144,896]{2,1,0:T(8,128)(2,1)S(1)} async-done(((bf16[4,144,896]{2,1,0:T(8,128)(2,1)}), bf16[4,144,896]{2,1,0:T(8,128)(2,1)S(1)}, u32[]{:S(2)}, u32[]{:S(2)}) %all-to-all-start) | async-done | bytes 1032224 | tf_op jit(solution)/shard_map/all_to_all | solution.py:140
  75.4 7.7 %collective-permute-done.2 = bf16[4,144,640]{2,1,0:T(8,128)(2,1)} collective-permute-done((bf16[4,144,640]{2,1,0:T(8,128)(2,1)}, bf16[4,144,640]{2,1,0:T(8,128)(2,1)}, u32[]{:S(2)}, u32[]{:S(2)}) %collective-permute-start.2) | collective-permute-done | bytes 737312 | tf_op jit(solution)/shard_map/ppermute | solution.py:112
  87.9 5.7 all-to-all-done.1
  110.5 47.3 %all-to-all-done.2 = bf16[4,144,2304]{2,1,0:T(8,128)(2,1)} async-done(((bf16[4,144,2304]{2,1,0:T(8,128)(2,1)}), bf16[4,144,2304]{2,1,0:T(8,128)(2,1)}, u32[]{:S(2)}, u32[]{:S(2)}) %all-to-all-start.2) | async-done | bytes 2654240 | tf_op jit(solution)/shard_map/all_to_all | solution.py:140
  179.2 10.0 %collective-permute-done.9 = bf16[4,144,256]{2,1,0:T(8,128)(2,1)S(1)} collective-permute-done((bf16[4,144,256]{2,1,0:T(8,128)(2,1)S(1)}, bf16[4,144,256]{2,1,0:T(8,128)(2,1)S(1)}, u32[]{:S(2)}, u32[]{:S(2)}) %collective-permute-start.9) | collective-permute-done | bytes 294944 | tf_op jit(solution)/shard_map/ppermute | solution.py:112
  193.0 10.9 %collective-permute-done.11 = bf16[4,144,256]{2,1,0:T(8,128)(2,1)S(1)} collective-permute-done((bf16[4,144,256]{2,1,0:T(8,128)(2,1)S(1)}, bf16[4,144,256]{2,1,0:T(8,128)(2,1)S(1)}, u32[]{:S(2)}, u32[]{:S(2)}) %collective-permute-start.11) | collective-permute-done | bytes 294944 | tf_op jit(solution)/shard_map/ppermute | solution.py:112
  216.6 7.8 %collective-permute-done.14 = bf16[64,2304]{1,0:T(8,128)(2,1)S(1)} collective-permute-done((bf16[64,2304]{1,0:T(8,128)(2,1)S(1)}, bf16[64,2304]{1,0:T(8,128)(2,1)S(1)}, u32[]{:S(2)}, u32[]{:S(2)}) %collective-permute-start.14) | collective-permute-done | bytes 294944 | tf_op jit(solution)/shard_map/ppermute | solution.py:101
  230.0 7.8 %collective-permute-done.15 = bf16[64,2304]{1,0:T(8,128)(2,1)S(1)} collective-permute-done((bf16[64,2304]{1,0:T(8,128)(2,1)S(1)}, bf16[64,2304]{1,0:T(8,128)(2,1)S(1)}, u32[]{:S(2)}, u32[]{:S(2)}) %collective-permute-start.15) | collective-permute-done | bytes 294944 | tf_op jit(solution)/shard_map/ppermute | solution.py:101
  245.8 7.3 %collective-permute-done.17 = bf16[64,2304]{1,0:T(8,128)(2,1)S(1)} collective-permute-done((bf16[64,2304]{1,0:T(8,128)(2,1)S(1)}, bf16[64,2304]{1,0:T(8,128)(2,1)S(1)}, u32[]{:S(2)}, u32[]{:S(2)}) %collective-permute-start.17) | collective-permute-done | bytes 294944 | tf_op jit(solution)/shard_map/ppermute | solution.py:101
  268.2 14.6 %all-gather.8.cloned.1.call-done = bf16[4,576,2304]{2,1,0:T(8,128)(2,1)} async-done(((bf16[4,144,2304]{2,1,0:T(8,128)(2,1)}), bf16[4,576,2304]{2,1,0:T(8,128)(2,1)}) %all-gather.8.cloned.1.call-update) | async-done | bytes 10616848 | tf_op jit(solution)/shard_map/all_gather | solution.py:175
  285.3 8.8 %gate_and_up.1 = (f32[512,1152]{1,0:T(8,128)S(1)}, f32[512,1152]{1,0:T(8,128)S(1)}, bf16[512,1152]{1,0:T(8,128)(2,1)S(1)}) custom-call(bf16[512,2304]{1,0:T(8,128)(2,1)S(1)} %constant_dynamic-update-slice_fusion.x_ref, bf16[2304,1152]{1,0:T(8,128)(2,1)S(1)} %bitcast.261, bf16[2304,2304]{1,0:T(8,128)(2,1)} %bitcast.245), custom_call_target="tpu_custom_call" | custom-call | flops 5435817984 | bytes 10616832 | tf_op jit(solution)/shard_map/gate_and_up/pallas_call | solution.py:621
  301.1 7.8 %collective-permute-done.22 = bf16[64,2304]{1,0:T(8,128)(2,1)S(1)} collective-permute-done((bf16[64,2304]{1,0:T(8,128)(2,1)S(1)}, bf16[64,2304]{1,0:T(8,128)(2,1)S(1)}, u32[]{:S(2)}, u32[]{:S(2)}) %collective-permute-start.22) | collective-permute-done | bytes 294944 | tf_op jit(solution)/shard_map/ppermute | solution.py:101
  314.5 8.3 %collective-permute-done.23 = bf16[64,2304]{1,0:T(8,128)(2,1)S(1)} collective-permute-done((bf16[64,2304]{1,0:T(8,128)(2,1)S(1)}, bf16[64,2304]{1,0:T(8,128)(2,1)S(1)}, u32[]{:S(2)}, u32[]{:S(2)}) %collective-permute-start.23) | collective-permute-done | bytes 294944 | tf_op jit(solution)/shard_map/ppermute | solution.py:101
  329.8 6.9 %collective-permute-done.26 = bf16[64,2304]{1,0:T(8,128)(2,1)S(1)} collective-permute-done((bf16[64,2304]{1,0:T(8,128)(2,1)S(1)}, bf16[64,2304]{1,0:T(8,128)(2,1)S(1)}, u32[]{:S(2)}, u32[]{:S(2)}) %collective-permute-start.26) | collective-permute-done | bytes 294944 | tf_op jit(solution)/shard_map/ppermute | solution.py:101
  350.9 6.3 gate_and_up_back.1
  357.1 8.3 %convolution_convert_fusion = bf16[2304,2304]{1,0:T(8,128)(2,1)} fusion(bf16[512,2304]{1,0:T(8,128)(2,1)S(1)} %copy-done.18, bf16[512,2304]{1,0:T(8,128)(2,1)S(1)} %gate_and_up_back.1), kind=kOutput, calls=%fused_computation | convolution fusion | flops 5441126400 | bytes 15335424 | tf_op jit(solution)/shard_map/dot_general | solution.py:591
  384.3 7.8 %collective-permute-done.31 = bf16[64,2304]{1,0:T(8,128)(2,1)S(1)} collective-permute-done((bf16[64,2304]{1,0:T(8,128)(2,1)S(1)}, bf16[64,2304]{1,0:T(8,128)(2,1)S(1)}, u32[]{:S(2)}, u32[]{:S(2)}) %collective-permute-start.31) | collective-permute-done | bytes 294944 | tf_op jit(solution)/shard_map/ppermute | solution.py:101
  398.1 6.7 %collective-permute-done.32 = bf16[64,2304]{1,0:T(8,128)(2,1)S(1)} collective-permute-done((bf16[64,2304]{1,0:T(8,128)(2,1)S(1)}, bf16[64,2304]{1,0:T(8,128)(2,1)S(1)}, u32[]{:S(2)}, u32[]{:S(2)}) %collective-permute-start.32) | collective-permute-done | bytes 294944 | tf_op jit(solution)/shard_map/ppermute | solution.py:101
  410.6 8.3 %collective-permute-done.34 = bf16[64,2304]{1,0:T(8,128)(2,1)S(1)} collective-permute-done((bf16[64,2304]{1,0:T(8,128)(2,1)S(1)}, bf16[64,2304]{1,0:T(8,128)(2,1)S(1)}, u32[]{:S(2)}, u32[]{:S(2)}) %collective-permute-start.34) | collective-permute-done | bytes 294944 | tf_op jit(solution)/shard_map/ppermute | solution.py:101
  424.2 7.2 %collective-permute-done.35 = bf16[64,2304]{1,0:T(8,128)(2,1)S(1)} collective-permute-done((bf16[64,2304]{1,0:T(8,128)(2,1)S(1)}, bf16[64,2304]{1,0:T(8,128)(2,1)S(1)}, u32[]{:S(2)}, u32[]{:S(2)}) %collective-permute-start.35) | collective-permute-done | bytes 294944 | tf_op jit(solution)/shard_map/ppermute | solution.py:101
  439.8 9.2 %attend_backward.1 = (f32[512,256]{1,0:T(8,128)}, f32[2048,256]{1,0:T(8,128)}, bf16[2048,256]{1,0:T(8,128)(2,1)}) custom-call(s32[1]{0:T(128)} %bitcast.core_ref, bf16[512,256]{1,0:T(8,128)(2,1)} %copy-done.23, bf16[2048,256]{1,0:T(8,128)(2,1)} %copy-done.16, bf16[2048,256]{1,0:T(8,128)(2,1)} %copy-done.15, s32[512,1]{1,0:T(8,128)} %copy-done.24, ...), custom_call_target="tpu_custom_call" | custom-call | flops 115000000512 | tf_op jit(solution)/shard_map/attend_backward/pallas_call | solution.py:555
  456.1 9.9 %collective-permute-done.39 = bf16[512,256]{1,0:T(8,128)(2,1)S(1)} collective-permute-done((bf16[512,256]{1,0:T(8,128)(2,1)S(1)}, bf16[512,256]{1,0:T(8,128)(2,1)S(1)}, u32[]{:S(2)}, u32[]{:S(2)}) %collective-permute-start.39) | collective-permute-done | bytes 262176 | tf_op jit(solution)/shard_map/ppermute | solution.py:112
  469.1 5.8 collective-permute-done.38
  503.0 6.5 copy.159
  509.5 42.0 %collective-permute-done.44 = bf16[64,2304]{1,0:T(8,128)(2,1)} collective-permute-done((bf16[64,2304]{1,0:T(8,128)(2,1)}, bf16[64,2304]{1,0:T(8,128)(2,1)}, u32[]{:S(2)}, u32[]{:S(2)}) %collective-permute-start.44) | collective-permute-done | bytes 294944 | tf_op jit(solution)/shard_map/ppermute | solution.py:101
  560.8 11.9 %all-to-all-start.4 = ((bf16[4,144,1152]{2,1,0:T(8,128)(2,1)}), bf16[4,144,1152]{2,1,0:T(8,128)(2,1)}, u32[]{:S(2)}, u32[]{:S(2)}) async-start(bf16[4,144,1152]{2,1,0:T(8,128)(2,1)} %reduce-scatter.6.cloned.1.call-done), calls=%async_computation.7 | async-start | bytes 2654208 | tf_op jit(solution)/shard_map/all_to_all | solution.py:140
  579.5 16.6 %adam_expand.1 = (f32[144,2,4608]{2,1,0:T(2,128)}, f32[144,2,4608]{2,1,0:T(2,128)}, f32[144,2,4608]{2,1,0:T(2,128)}, f32[144,2,4608]{2,1,0:T(2,128)}) custom-call(bf16[4,144,2304]{2,1,0:T(8,128)(2,1)S(1)} %copy-done.7, f32[144,2,4608]{2,1,0:T(2,128)S(1)} %copy-done.3, f32[144,2,4608]{2,1,0:T(2,128)S(1)} %copy-done.26, f32[144,2,4608]{2,1,0:T(2,128)} %refs_2_.1), custom_call_target="tpu_custom_call" | custom-call | flops 69000003584 | tf_op jit(solution)/shard_map/adam_expand/pallas_call | solution.py:312
  597.5 8.2 %all-to-all-done.4.grad_ref = bf16[4,144,1152]{2,1,0:T(8,128)(2,1)} async-done(((bf16[4,144,1152]{2,1,0:T(8,128)(2,1)}), bf16[4,144,1152]{2,1,0:T(8,128)(2,1)}, u32[]{:S(2)}, u32[]{:S(2)}) %all-to-all-start.4) | async-done | bytes 1327136 | tf_op jit(solution)/shard_map/all_to_all | solution.py:140
  613.5 8.3 %adam_shrink.1 = (f32[144,4608]{1,0:T(8,128)}, f32[144,4608]{1,0:T(8,128)}, f32[144,4608]{1,0:T(8,128)}, f32[144,4608]{1,0:T(8,128)}) custom-call(bf16[4,144,1152]{2,1,0:T(8,128)(2,1)} %all-to-all-done.4.grad_ref, f32[144,4608]{1,0:T(8,128)S(1)} %bitcast.256, f32[144,4608]{1,0:T(8,128)S(1)} %bitcast.262, f32[144,4608]{1,0:T(8,128)S(1)} %bitcast.263), custom_call_target="tpu_custom_call" | custom-call | flops 46000001024 | tf_op jit(solution)/shard_map/adam_shrink/pallas_call | solution.py:312
  621.8 14.0 %all-to-all-done.5 = bf16[4,144,896]{2,1,0:T(8,128)(2,1)} async-done(((bf16[4,144,896]{2,1,0:T(8,128)(2,1)}), bf16[4,144,896]{2,1,0:T(8,128)(2,1)}, u32[]{:S(2)}, u32[]{:S(2)}) %all-to-all-start.5) | async-done | bytes 1032224 | tf_op jit(solution)/shard_map/all_to_all | solution.py:140
  (418 shorter events, 270.1 us)
Async XLA Ops:
  14.1 46.4 %all-to-all-start = ((bf16[4,144,896]{2,1,0:T(8,128)(2,1)}), bf16[4,144,896]{2,1,0:T(8,128)(2,1)S(1)}, u32[]{:S(2)}, u32[]{:S(2)}) async-start(bf16[4,144,896]{2,1,0:T(8,128)(2,1)} %maximum_select_fusion.1), calls=%async_computation | async-start | bytes 2064384 | tf_op jit(solution)/shard_map/all_to_all | solution.py:140
  20.3 49.0 %all-gather.4.cloned.1.call-start = ((), (), s32[]{:S(2)}) async-start(), calls=%async_computation.9 | async-start | bytes 1474560 | tf_op jit(solution)/shard_map/all_gather | solution.py:706
  60.5 33.0 %all-to-all-start.1 = ((bf16[4,144,1152]{2,1,0:T(8,128)(2,1)}), bf16[4,144,1152]{2,1,0:T(8,128)(2,1)}, u32[]{:S(2)}, u32[]{:S(2)}) async-start(bf16[4,144,1152]{2,1,0:T(8,128)(2,1)} %get-tuple-element.66), calls=%async_computation.1 | async-start | bytes 2654208 | tf_op jit(solution)/shard_map/all_to_all | solution.py:140
  66.1 16.9 %collective-permute-start.2 = (bf16[4,144,640]{2,1,0:T(8,128)(2,1)}, bf16[4,144,640]{2,1,0:T(8,128)(2,1)}, u32[]{:S(2)}, u32[]{:S(2)}) collective-permute-start(bf16[4,144,640]{2,1,0:T(8,128)(2,1)} %slice.180), channel_id=1, source_target_pairs={{0,2},{1,5},{2,0},{3,7},{4,6},{5,1},{6,4},{7,3},{8,10},{9,13},{10,... | collective-permute-start | bytes 2211848 | tf_op jit(solution)/shard_map/ppermute | solution.py:112
  69.3 18.4 %collective-permute-start = (bf16[256,2304]{1,0:T(8,128)(2,1)}, bf16[256,2304]{1,0:T(8,128)(2,1)S(1)}, u32[]{:S(2)}, u32[]{:S(2)}) collective-permute-start(bf16[256,2304]{1,0:T(8,128)(2,1)} %all-gather.4.cloned.1.call-done), channel_id=1, source_target_pairs={{0,1},{1,0},{2,3},{3,2},{4,5},{5,4},{6,7},{7,6},{8,9},{9,8},{10,11... | collective-permute-start | bytes 3538952 | tf_op jit(solution)/shard_map/ppermute | solution.py:104
  69.4 16.6 %collective-permute-start.3 = (bf16[4,144,640]{2,1,0:T(8,128)(2,1)}, bf16[4,144,640]{2,1,0:T(8,128)(2,1)S(1)}, u32[]{:S(2)}, u32[]{:S(2)}) collective-permute-start(bf16[4,144,640]{2,1,0:T(8,128)(2,1)} %slice.180), channel_id=1, source_target_pairs={{0,4},{1,3},{2,6},{3,1},{4,0},{5,7},{6,2},{7,5},{8,12},{9,11},{10,... | collective-permute-start | bytes 2211848 | tf_op jit(solution)/shard_map/ppermute | solution.py:112
  83.0 18.7 %collective-permute-start.4 = (bf16[4,144,640]{2,1,0:T(8,128)(2,1)}, bf16[4,144,640]{2,1,0:T(8,128)(2,1)S(1)}, u32[]{:S(2)}, u32[]{:S(2)}) collective-permute-start(bf16[4,144,640]{2,1,0:T(8,128)(2,1)} %collective-permute-done.2), channel_id=1, source_target_pairs={{0,4},{1,3},{2,6},{3,1},{4,0},{5,7},{6,2},{7,5},{8,12},{9,11},{10,... | collective-permute-start | bytes 2211848 | tf_op jit(solution)/shard_map/ppermute | solution.py:112
  93.5 64.4 %all-to-all-start.2 = ((bf16[4,144,2304]{2,1,0:T(8,128)(2,1)}), bf16[4,144,2304]{2,1,0:T(8,128)(2,1)}, u32[]{:S(2)}, u32[]{:S(2)}) async-start(bf16[4,144,2304]{2,1,0:T(8,128)(2,1)} %pad_maximum_fusion.1), calls=%async_computation.2 | async-start | bytes 5308416 | tf_op jit(solution)/shard_map/all_to_all | solution.py:140
  98.1 166.9 %all-gather.6.cloned.1.call-start = ((), (), s32[]{:S(2)}) async-start(), calls=%async_computation.10 | async-start | bytes 6635520 | tf_op jit(solution)/shard_map/all_gather | solution.py:175
  98.7 184.1 %all-gather.8.cloned.1.call-start = ((), (), s32[]{:S(2)}) async-start(), calls=%async_computation.11 | async-start | bytes 13271040 | tf_op jit(solution)/shard_map/all_gather | solution.py:175
  157.9 328.7 %reduce-scatter.8.cloned.1.call-start = ((), (), s32[]{:S(2)}) async-start(), calls=%async_computation.14 | async-start | bytes 13271040 | tf_op jit(solution)/shard_map/reduce_scatter | solution.py:180
  175.7 13.5 %collective-permute-start.9 = (bf16[4,144,256]{2,1,0:T(8,128)(2,1)S(1)}, bf16[4,144,256]{2,1,0:T(8,128)(2,1)S(1)}, u32[]{:S(2)}, u32[]{:S(2)}) collective-permute-start(bf16[4,144,256]{2,1,0:T(8,128)(2,1)S(1)} %slice.193), channel_id=1, source_target_pairs={{0,2},{1,5},{2,0},{3,7},{4,6},{5,1},{6,4},{7,3},{8,10},{9,13},{10,... | collective-permute-start | bytes 884744 | tf_op jit(solution)/shard_map/ppermute | solution.py:112
  176.4 27.5 %collective-permute-start.8 = (bf16[2048,256]{1,0:T(8,128)(2,1)S(1)}, bf16[2048,256]{1,0:T(8,128)(2,1)S(1)}, u32[]{:S(2)}, u32[]{:S(2)}) collective-permute-start(bf16[2048,256]{1,0:T(8,128)(2,1)S(1)} %bitcast.291), channel_id=1, source_target_pairs={{0,1},{1,0},{2,3},{3,2},{4,5},{5,4},{6,7},{7,6},{8,9},{9,8},{10,11... | collective-permute-start | bytes 3145736 | tf_op jit(solution)/shard_map/ppermute | solution.py:104
  176.5 16.4 %collective-permute-start.10 = (bf16[4,144,256]{2,1,0:T(8,128)(2,1)S(1)}, bf16[4,144,256]{2,1,0:T(8,128)(2,1)S(1)}, u32[]{:S(2)}, u32[]{:S(2)}) collective-permute-start(bf16[4,144,256]{2,1,0:T(8,128)(2,1)S(1)} %slice.193), channel_id=1, source_target_pairs={{0,4},{1,3},{2,6},{3,1},{4,0},{5,7},{6,2},{7,5},{8,12},{9,11},{10,... | collective-permute-start | bytes 884744 | tf_op jit(solution)/shard_map/ppermute | solution.py:112
  189.2 14.7 %collective-permute-start.11 = (bf16[4,144,256]{2,1,0:T(8,128)(2,1)S(1)}, bf16[4,144,256]{2,1,0:T(8,128)(2,1)S(1)}, u32[]{:S(2)}, u32[]{:S(2)}) collective-permute-start(bf16[4,144,256]{2,1,0:T(8,128)(2,1)S(1)} %collective-permute-done.9), channel_id=1, source_target_pairs={{0,4},{1,3},{2,6},{3,1},{4,0},{5,7},{6,2},{7,5},{8,12},{9,11},{10,... | collective-permute-start | bytes 884744 | tf_op jit(solution)/shard_map/ppermute | solution.py:112
  215.8 14.2 %collective-permute-start.13 = (bf16[64,2304]{1,0:T(8,128)(2,1)S(1)}, bf16[64,2304]{1,0:T(8,128)(2,1)S(1)}, u32[]{:S(2)}, u32[]{:S(2)}) collective-permute-start(bf16[64,2304]{1,0:T(8,128)(2,1)S(1)} %get-tuple-element.170), channel_id=1, source_target_pairs={{0,8},{8,0},{16,24},{24,16},{1,9},{9,1},{17,25},{25,17},{2,10},{10... | collective-permute-start | bytes 884744 | tf_op jit(solution)/shard_map/ppermute | solution.py:101
  242.9 14.4 %collective-permute-start.16 = (bf16[64,2304]{1,0:T(8,128)(2,1)S(1)}, bf16[64,2304]{1,0:T(8,128)(2,1)S(1)}, u32[]{:S(2)}, u32[]{:S(2)}) collective-permute-start(bf16[64,2304]{1,0:T(8,128)(2,1)S(1)} %get-tuple-element.154), channel_id=1, source_target_pairs={{0,8},{8,0},{16,24},{24,16},{1,9},{9,1},{17,25},{25,17},{2,10},{10... | collective-permute-start | bytes 884744 | tf_op jit(solution)/shard_map/ppermute | solution.py:101
  300.6 13.9 %collective-permute-start.21 = (bf16[64,2304]{1,0:T(8,128)(2,1)S(1)}, bf16[64,2304]{1,0:T(8,128)(2,1)S(1)}, u32[]{:S(2)}, u32[]{:S(2)}) collective-permute-start(bf16[64,2304]{1,0:T(8,128)(2,1)S(1)} %get-tuple-element.168), channel_id=1, source_target_pairs={{0,8},{8,0},{16,24},{24,16},{1,9},{9,1},{17,25},{25,17},{2,10},{10... | collective-permute-start | bytes 884744 | tf_op jit(solution)/shard_map/ppermute | solution.py:101
  309.0 13.7 %collective-permute-start.23 = (bf16[64,2304]{1,0:T(8,128)(2,1)S(1)}, bf16[64,2304]{1,0:T(8,128)(2,1)S(1)}, u32[]{:S(2)}, u32[]{:S(2)}) collective-permute-start(bf16[64,2304]{1,0:T(8,128)(2,1)S(1)} %fusion.44), channel_id=1, source_target_pairs={{0,24},{8,16},{16,8},{24,0},{1,25},{9,17},{17,9},{25,1},{2,26},{10... | collective-permute-start | bytes 884744 | tf_op jit(solution)/shard_map/ppermute | solution.py:101
  326.3 15.0 %collective-permute-start.25 = (bf16[64,2304]{1,0:T(8,128)(2,1)S(1)}, bf16[64,2304]{1,0:T(8,128)(2,1)S(1)}, u32[]{:S(2)}, u32[]{:S(2)}) collective-permute-start(bf16[64,2304]{1,0:T(8,128)(2,1)S(1)} %get-tuple-element.150), channel_id=1, source_target_pairs={{0,8},{8,0},{16,24},{24,16},{1,9},{9,1},{17,25},{25,17},{2,10},{10... | collective-permute-start | bytes 884744 | tf_op jit(solution)/shard_map/ppermute | solution.py:101
  365.5 191.7 %reduce-scatter.6.cloned.1.call-start = ((), (), s32[]{:S(2)}) async-start(), calls=%async_computation.13 | async-start | bytes 6635520 | tf_op jit(solution)/shard_map/reduce_scatter | solution.py:180
  382.2 15.9 %collective-permute-start.30 = (bf16[64,2304]{1,0:T(8,128)(2,1)S(1)}, bf16[64,2304]{1,0:T(8,128)(2,1)S(1)}, u32[]{:S(2)}, u32[]{:S(2)}) collective-permute-start(bf16[64,2304]{1,0:T(8,128)(2,1)S(1)} %get-tuple-element.164), channel_id=1, source_target_pairs={{0,8},{8,0},{16,24},{24,16},{1,9},{9,1},{17,25},{25,17},{2,10},{10... | collective-permute-start | bytes 884744 | tf_op jit(solution)/shard_map/ppermute | solution.py:101
  392.1 12.8 %collective-permute-start.32 = (bf16[64,2304]{1,0:T(8,128)(2,1)S(1)}, bf16[64,2304]{1,0:T(8,128)(2,1)S(1)}, u32[]{:S(2)}, u32[]{:S(2)}) collective-permute-start(bf16[64,2304]{1,0:T(8,128)(2,1)S(1)} %fusion.42), channel_id=1, source_target_pairs={{0,24},{8,16},{16,8},{24,0},{1,25},{9,17},{17,9},{25,1},{2,26},{10... | collective-permute-start | bytes 884744 | tf_op jit(solution)/shard_map/ppermute | solution.py:101
  408.8 15.4 %collective-permute-start.33 = (bf16[64,2304]{1,0:T(8,128)(2,1)S(1)}, bf16[64,2304]{1,0:T(8,128)(2,1)S(1)}, u32[]{:S(2)}, u32[]{:S(2)}) collective-permute-start(bf16[64,2304]{1,0:T(8,128)(2,1)S(1)} %get-tuple-element.146), channel_id=1, source_target_pairs={{0,8},{8,0},{16,24},{24,16},{1,9},{9,1},{17,25},{25,17},{2,10},{10... | collective-permute-start | bytes 884744 | tf_op jit(solution)/shard_map/ppermute | solution.py:101
  455.8 19.1 %collective-permute-start.38 = (bf16[512,256]{1,0:T(8,128)(2,1)S(1)}, bf16[512,256]{1,0:T(8,128)(2,1)S(1)}, u32[]{:S(2)}, u32[]{:S(2)}) collective-permute-start(bf16[512,256]{1,0:T(8,128)(2,1)S(1)} %get-tuple-element.178), channel_id=1, source_target_pairs={{0,4},{1,3},{2,6},{3,1},{4,0},{5,7},{6,2},{7,5},{8,12},{9,11},{10,... | collective-permute-start | bytes 786440 | tf_op jit(solution)/shard_map/ppermute | solution.py:112
  478.6 75.1 %collective-permute-start.24 = (bf16[64,2304]{1,0:T(8,128)(2,1)}, bf16[64,2304]{1,0:T(8,128)(2,1)}, u32[]{:S(2)}, u32[]{:S(2)}) collective-permute-start(bf16[64,2304]{1,0:T(8,128)(2,1)} %get-tuple-element.182), channel_id=1, source_target_pairs={{0,1},{1,0},{2,3},{3,2},{4,5},{5,4},{6,7},{7,6},{8,9},{9,8},{10,11... | collective-permute-start | bytes 884744 | tf_op jit(solution)/shard_map/ppermute | solution.py:104
  486.0 23.5 %collective-permute-start.42 = (bf16[64,2304]{1,0:T(8,128)(2,1)}, bf16[64,2304]{1,0:T(8,128)(2,1)}, u32[]{:S(2)}, u32[]{:S(2)}) collective-permute-start(bf16[64,2304]{1,0:T(8,128)(2,1)} %get-tuple-element.162), channel_id=1, source_target_pairs={{0,8},{8,0},{16,24},{24,16},{1,9},{9,1},{17,25},{25,17},{2,10},{10... | collective-permute-start | bytes 884744 | tf_op jit(solution)/shard_map/ppermute | solution.py:101
  486.6 72.7 %all-to-all-start.3 = ((bf16[4,144,2304]{2,1,0:T(8,128)(2,1)}), bf16[4,144,2304]{2,1,0:T(8,128)(2,1)S(1)}, u32[]{:S(2)}, u32[]{:S(2)}) async-start(bf16[4,144,2304]{2,1,0:T(8,128)(2,1)} %reduce-scatter.8.cloned.1.call-done), calls=%async_computation.6 | async-start | bytes 5308416 | tf_op jit(solution)/shard_map/all_to_all | solution.py:140
  491.3 106.2 %reduce-scatter.4.cloned.1.call-start = ((), (), s32[]{:S(2)}) async-start(), calls=%async_computation.12 | async-start | bytes 5160960 | tf_op jit(solution)/shard_map/reduce_scatter | solution.py:180
  497.0 54.6 %collective-permute-start.44 = (bf16[64,2304]{1,0:T(8,128)(2,1)}, bf16[64,2304]{1,0:T(8,128)(2,1)}, u32[]{:S(2)}, u32[]{:S(2)}) collective-permute-start(bf16[64,2304]{1,0:T(8,128)(2,1)} %fusion.40), channel_id=1, source_target_pairs={{0,24},{8,16},{16,8},{24,0},{1,25},{9,17},{17,9},{25,1},{2,26},{10... | collective-permute-start | bytes 884744 | tf_op jit(solution)/shard_map/ppermute | solution.py:101
  560.8 44.9 %all-to-all-start.4 = ((bf16[4,144,1152]{2,1,0:T(8,128)(2,1)}), bf16[4,144,1152]{2,1,0:T(8,128)(2,1)}, u32[]{:S(2)}, u32[]{:S(2)}) async-start(bf16[4,144,1152]{2,1,0:T(8,128)(2,1)} %reduce-scatter.6.cloned.1.call-done), calls=%async_computation.7 | async-start | bytes 2654208 | tf_op jit(solution)/shard_map/all_to_all | solution.py:140
  605.7 30.1 %all-to-all-start.5 = ((bf16[4,144,896]{2,1,0:T(8,128)(2,1)}), bf16[4,144,896]{2,1,0:T(8,128)(2,1)}, u32[]{:S(2)}, u32[]{:S(2)}) async-start(bf16[4,144,896]{2,1,0:T(8,128)(2,1)} %reduce-scatter.4.cloned.1.call-done), calls=%async_computation.8 | async-start | bytes 2064384 | tf_op jit(solution)/shard_map/all_to_all | solution.py:140
  (112 other events, 1414.6 us)
Sparse Core Ops, SparseCore 0:
  23.3 45.9 all-gather.3
Sparse Core Ops, SparseCore 1:
  100.4 64.4 all-gather.5
  166.6 116.1 all-gather.7
  365.6 109.5 reduce-scatter.7
  478.7 63.6 reduce-scatter.5
  545.5 52.0 reduce-scatter.3
where the time goes:
time: 663 us; the launch traced here: 657 us
  waiting for transfers between devices  330 us (50%)
  starting transfers between devices  106 us (16%)
  Pallas kernels  64.9 us (10%)
  local copies, waits for them, and re-layouts  56.5 us (9%)
  matrix products  44.9 us (7%)
  other arithmetic  37.2 us (6%)
  between operations  17.5 us (3%)
    ppermute x21, waiting for transfers between devices, along(): return lax.ppermute(value, 'line', pairs)  139 us
    all_to_all x6, waiting for transfers between devices, line_swap(): lax.all_to_all(blocks, 'line', split_axis=0, concat_axis=0, tiled=True)  106 us
    ppermute x12, waiting for transfers between devices, within(): return lax.ppermute(value, ('place', 'head'), pairs)  53.8 us
    ppermute x21, starting transfers between devices, along(): return lax.ppermute(value, 'line', pairs)  45.1 us
    all_to_all x6, starting transfers between devices, line_swap(): lax.all_to_all(blocks, 'line', split_axis=0, concat_axis=0, tiled=True)  35.9 us
    unnamed x169, local copies, waits for them, and re-layouts  35 us
    pallas_call x3, Pallas kernels, adam_call(): pl.pallas_call(kernel, out_shape=[jax.ShapeDtypeStruct(states[0].shape, F...  30.3 us
    dot_general x10, matrix products, dot_last(): return lax.dot_general(left, right, LAST, preferred_element_type=F32)  23.1 us
  transfers between devices with their start and end apart: 61, of which 41 were waited for; matrix products, arithmetic and copies ran while one was open for 14% of the time, Pallas kernels for 7%

commit v1 on v0

--- a/solution.py
+++ b/solution.py
@@ -457,7 +457,7 @@
 
 
 PEAK = 1.15e15
-ATTEND_WEIGHT = 30
+ATTEND_WEIGHT = 45
 ATTEND_BACK_WEIGHT = 100
 
 
@@ -783,7 +783,9 @@
     grad_out = own_out.astype(F32)
     grad_feed, gain_four = norm_back(feed_sum, gains_all[3], grad_out)
     grad_feed_line = grid.token_gather(grad_feed.astype(BF16))
-    grad_both_b = gate_and_up_back(grad_feed_line, gate_act, up_act, up_shrink_full)
+    shrink_terms = dot_rows(grad_feed_line, inner_b).astype(BF16)
+    shrink_sums = grid.bulk_sum(shrink_terms)
+    grad_both_b = gate_and_up_back(after(grad_feed_line, shrink_terms), gate_act, up_act, up_shrink_full)
     expand_terms = dot_rows(normed_two_line, grad_both_b).astype(BF16)
     expand_sums = grid.bulk_sum(expand_terms)
     grad_both_b = after(grad_both_b, expand_terms)
@@ -791,8 +793,6 @@
         (grad_both_b[:, :units], gate_full), (grad_both_b[:, units:], up_full)
     )
     grad_two = grid.token_reduce(*grad_two_parts)
-    shrink_terms = dot_rows(grad_feed_line, after(inner_b, grad_two)).astype(BF16)
-    shrink_sums = grid.bulk_sum(shrink_terms)
 
     grad_first_norm, gain_three = norm_back(first_sum, gains_all[2], grad_two)
     grad_first = grad_out + grad_first_norm
@@ -812,21 +812,21 @@
     grad_query_pre = rotate(grad_query, cosine, -sine_table)
     grad_pair_pre = jnp.where(core == 0, rotate(pair_grad, cosine, -sine_table), pair_grad)
     grad_proj_b = jnp.concatenate([grad_query_pre, grad_pair_pre], axis=1).astype(BF16)
-    own_part, other_part = halves_last((grad_proj_b, attend_full))
+    shrink_back = grid.line_swap(after(shrink_sums, grad_attend_line))
+    own_part, other_part = halves_last((after(grad_proj_b, shrink_back), attend_full))
     gain_one = jnp.sum(own_part * normed_plain[:half], axis=0) + jnp.sum(
         other_part.astype(F32) * normed_plain[half:], axis=0
     )
     grad_normed = grid.token_reduce(own_part, other_part)
     own_hidden_grad = last_grad(own_in, gains_all[0], grad_normed, grad_first)
-    expand_back = grid.line_swap(expand_sums)
+    expand_back = grid.line_swap(after(expand_sums, shrink_back))
 
     gain_terms = jnp.stack([gain_one, gain_two, gain_three, gain_four], axis=1)
     gain_terms = jnp.pad(gain_terms, ((0, 0), (2 * head_width, TILE - gain_count)))
     attend_terms = dot_rows(normed_line, jnp.pad(grad_proj_b, ((0, 0), (0, TILE)))) + gain_terms
     joined_terms = jnp.concatenate([attend_terms.astype(BF16), output_terms], axis=1)
     joined_sums = grid.bulk_sum(joined_terms)
-    shrink_back = grid.line_swap(after(shrink_sums, expand_back))
-    joined = grid.line_swap(after(joined_sums, shrink_back))
+    joined = grid.line_swap(after(joined_sums, expand_back))
     attend_line = joined[..., :attend_columns]
     output_back = group_return(joined[..., attend_columns:])
     attend_back = group_return(attend_line)

time: 663 us -> 643 us (0.970)
  starting transfers between devices: 106 us -> 84.6 us
    reduce_scatter x3, waiting for transfers between devices: 1.47 us -> 35.3 us  [bulk_sum(): return lax.psum_scatter(shaped, 'place', scatter_dimension=1, tiled=True)]
    ppermute x21, waiting for transfers between devices: 139 us -> 118 us  [along(): return lax.ppermute(value, 'line', pairs)]
    all_to_all x6, waiting for transfers between devices: 106 us -> 88.5 us  [line_swap(): lax.all_to_all(blocks, 'line', split_axis=0, concat_axis=0, tiled=True)]
    ppermute x12, waiting for transfers between devices: 53.8 us -> 40.3 us  [within(): return lax.ppermute(value, ('place', 'head'), pairs)]
    all_to_all x6, starting transfers between devices: 35.9 us -> 26.4 us  [line_swap(): lax.all_to_all(blocks, 'line', split_axis=0, concat_axis=0, tiled=True)]
    all_gather x2, waiting for transfers between devices: 14.6 us -> 23 us  [bulk_spread(): full = lax.all_gather(own, 'place', axis=1, tiled=True)]
    ppermute x21, starting transfers between devices: 45.1 us -> 37.6 us  [along(): return lax.ppermute(value, 'line', pairs)]
  transfers between devices with their start and end apart: 61 -> 61, of which waited for: 41 -> 43; matrix products, arithmetic and copies ran while one was open for 14% -> 15% of each run, Pallas kernels for 7% -> 8%
where the time goes in v1:
time: 643 us; the launch traced here: 635 us
  waiting for transfers between devices  326 us (51%)
  starting transfers between devices  84.6 us (13%)
  Pallas kernels  63.6 us (10%)
  local copies, waits for them, and re-layouts  62.5 us (10%)
  matrix products  43.2 us (7%)
  other arithmetic  37.7 us (6%)
  between operations  17.5 us (3%)
    ppermute x21, waiting for transfers between devices, along(): return lax.ppermute(value, 'line', pairs)  118 us
    all_to_all x6, waiting for transfers between devices, line_swap(): lax.all_to_all(blocks, 'line', split_axis=0, concat_axis=0, tiled=True)  88.5 us
    ppermute x12, waiting for transfers between devices, within(): return lax.ppermute(value, ('place', 'head'), pairs)  40.3 us
    ppermute x21, starting transfers between devices, along(): return lax.ppermute(value, 'line', pairs)  37.6 us
    unnamed x169, local copies, waits for them, and re-layouts  37.3 us
    reduce_scatter x3, waiting for transfers between devices, bulk_sum(): return lax.psum_scatter(shaped, 'place', scatter_dimension=1, tiled=True)  35.3 us
    pallas_call x3, Pallas kernels, adam_call(): pl.pallas_call(kernel, out_shape=[jax.ShapeDtypeStruct(states[0].shape, F...  28.6 us
    all_to_all x6, starting transfers between devices, line_swap(): lax.all_to_all(blocks, 'line', split_axis=0, concat_axis=0, tiled=True)  26.4 us
  transfers between devices with their start and end apart: 61, of which 43 were waited for; matrix products, arithmetic and copies ran while one was open for 15% of the time, Pallas kernels for 8%

profile of v1, /device:TPU:0, one launch (start us, length us, event | category | flops | bytes accessed | tf_op | source)
XLA Modules:
  0.0 634.7 jit_solution(5912759041753370149)
XLA Ops:
  14.1 6.2 all-to-all-start
  24.1 6.2 pack_expand.1
  31.4 29.1 %all-to-all-done = bf16[4,144,896]{2,1,0:T(8,128)(2,1)S(1)} async-done(((bf16[4,144,896]{2,1,0:T(8,128)(2,1)}), bf16[4,144,896]{2,1,0:T(8,128)(2,1)S(1)}, u32[]{:S(2)}, u32[]{:S(2)}) %all-to-all-start) | async-done | bytes 1032224 | tf_op jit(solution)/shard_map/all_to_all | solution.py:140
  77.8 6.6 %collective-permute-done.2 = bf16[4,144,640]{2,1,0:T(8,128)(2,1)S(1)} collective-permute-done((bf16[4,144,640]{2,1,0:T(8,128)(2,1)}, bf16[4,144,640]{2,1,0:T(8,128)(2,1)S(1)}, u32[]{:S(2)}, u32[]{:S(2)}) %collective-permute-start.2) | collective-permute-done | bytes 737312 | tf_op jit(solution)/shard_map/ppermute | solution.py:112
  127.9 32.0 %all-to-all-done.2 = bf16[4,144,2304]{2,1,0:T(8,128)(2,1)S(1)} async-done(((bf16[4,144,2304]{2,1,0:T(8,128)(2,1)}), bf16[4,144,2304]{2,1,0:T(8,128)(2,1)S(1)}, u32[]{:S(2)}, u32[]{:S(2)}) %all-to-all-start.2) | async-done | bytes 2654240 | tf_op jit(solution)/shard_map/all_to_all | solution.py:140
  173.9 9.4 %collective-permute-done.11 = bf16[4,144,256]{2,1,0:T(8,128)(2,1)S(1)} collective-permute-done((bf16[4,144,256]{2,1,0:T(8,128)(2,1)S(1)}, bf16[4,144,256]{2,1,0:T(8,128)(2,1)S(1)}, u32[]{:S(2)}, u32[]{:S(2)}) %collective-permute-start.11) | collective-permute-done | bytes 294944 | tf_op jit(solution)/shard_map/ppermute | solution.py:112
  195.9 7.8 %collective-permute-done.14 = bf16[64,2304]{1,0:T(8,128)(2,1)S(1)} collective-permute-done((bf16[64,2304]{1,0:T(8,128)(2,1)S(1)}, bf16[64,2304]{1,0:T(8,128)(2,1)S(1)}, u32[]{:S(2)}, u32[]{:S(2)}) %collective-permute-start.14) | collective-permute-done | bytes 294944 | tf_op jit(solution)/shard_map/ppermute | solution.py:101
  204.9 10.9 %collective-permute-done.13 = bf16[64,2304]{1,0:T(8,128)(2,1)S(1)} collective-permute-done((bf16[64,2304]{1,0:T(8,128)(2,1)S(1)}, bf16[64,2304]{1,0:T(8,128)(2,1)S(1)}, u32[]{:S(2)}, u32[]{:S(2)}) %collective-permute-start.13) | collective-permute-done | bytes 294944 | tf_op jit(solution)/shard_map/ppermute | solution.py:101
  221.9 7.5 %collective-permute-done.17 = bf16[64,2304]{1,0:T(8,128)(2,1)S(1)} collective-permute-done((bf16[64,2304]{1,0:T(8,128)(2,1)S(1)}, bf16[64,2304]{1,0:T(8,128)(2,1)S(1)}, u32[]{:S(2)}, u32[]{:S(2)}) %collective-permute-start.17) | collective-permute-done | bytes 294944 | tf_op jit(solution)/shard_map/ppermute | solution.py:101
  234.9 7.3 %collective-permute-done.18 = bf16[64,2304]{1,0:T(8,128)(2,1)S(1)} collective-permute-done((bf16[64,2304]{1,0:T(8,128)(2,1)S(1)}, bf16[64,2304]{1,0:T(8,128)(2,1)S(1)}, u32[]{:S(2)}, u32[]{:S(2)}) %collective-permute-start.18) | collective-permute-done | bytes 294944 | tf_op jit(solution)/shard_map/ppermute | solution.py:101
  246.7 23.0 %all-gather.8.cloned.1.call-done = bf16[4,576,2304]{2,1,0:T(8,128)(2,1)} async-done(((bf16[4,144,2304]{2,1,0:T(8,128)(2,1)}), bf16[4,576,2304]{2,1,0:T(8,128)(2,1)}) %all-gather.8.cloned.1.call-update) | async-done | bytes 10616848 | tf_op jit(solution)/shard_map/all_gather | solution.py:175
  273.8 8.5 %gate_and_up.1 = (f32[512,1152]{1,0:T(8,128)S(1)}, f32[512,1152]{1,0:T(8,128)S(1)}, bf16[512,1152]{1,0:T(8,128)(2,1)S(1)}) custom-call(bf16[512,2304]{1,0:T(8,128)(2,1)S(1)} %copy-done.21, bf16[2304,1152]{1,0:T(8,128)(2,1)S(1)} %bitcast.260, bf16[2304,2304]{1,0:T(8,128)(2,1)} %bitcast.245), custom_call_target="tpu_custom_call" | custom-call | flops 5435817984 | bytes 10616832 | tf_op jit(solution)/shard_map/gate_and_up/pallas_call | solution.py:621
  289.4 7.8 %collective-permute-done.22 = bf16[64,2304]{1,0:T(8,128)(2,1)S(1)} collective-permute-done((bf16[64,2304]{1,0:T(8,128)(2,1)S(1)}, bf16[64,2304]{1,0:T(8,128)(2,1)S(1)}, u32[]{:S(2)}, u32[]{:S(2)}) %collective-permute-start.22) | collective-permute-done | bytes 294944 | tf_op jit(solution)/shard_map/ppermute | solution.py:101
  302.7 8.3 %collective-permute-done.23 = bf16[64,2304]{1,0:T(8,128)(2,1)S(1)} collective-permute-done((bf16[64,2304]{1,0:T(8,128)(2,1)S(1)}, bf16[64,2304]{1,0:T(8,128)(2,1)S(1)}, u32[]{:S(2)}, u32[]{:S(2)}) %collective-permute-start.23) | collective-permute-done | bytes 294944 | tf_op jit(solution)/shard_map/ppermute | solution.py:101
  318.1 6.9 %collective-permute-done.26 = bf16[64,2304]{1,0:T(8,128)(2,1)S(1)} collective-permute-done((bf16[64,2304]{1,0:T(8,128)(2,1)S(1)}, bf16[64,2304]{1,0:T(8,128)(2,1)S(1)}, u32[]{:S(2)}, u32[]{:S(2)}) %collective-permute-start.26) | collective-permute-done | bytes 294944 | tf_op jit(solution)/shard_map/ppermute | solution.py:101
  350.4 6.4 %gate_and_up_back.1 = bf16[512,2304]{1,0:T(8,128)(2,1)S(1)} custom-call(bf16[512,2304]{1,0:T(8,128)(2,1)S(1)} %pad_maximum_fusion.3.feed_ref, f32[512,1152]{1,0:T(8,128)S(1)} %get-tuple-element.83.gate_ref, f32[512,1152]{1,0:T(8,128)S(1)} %copy-done.8, bf16[2304,2304]{1,0:T(8,128)(2,1)S(1)} %bitcast.248), custom_call_target="tpu_custom_call" | custom-call | flops 2717908992 | bytes 5308416 | tf_op jit(solution)/shard_map/gate_and_up_back/pallas_call | solution.py:655
  356.9 8.3 %convolution_convert_fusion = bf16[2304,2304]{1,0:T(8,128)(2,1)} fusion(bf16[512,2304]{1,0:T(8,128)(2,1)S(1)} %copy-done.22, bf16[512,2304]{1,0:T(8,128)(2,1)S(1)} %gate_and_up_back.1), kind=kOutput, calls=%fused_computation | convolution fusion | flops 5441126400 | bytes 15335424 | tf_op jit(solution)/shard_map/dot_general | solution.py:591
  378.6 7.8 %collective-permute-done.31 = bf16[64,2304]{1,0:T(8,128)(2,1)S(1)} collective-permute-done((bf16[64,2304]{1,0:T(8,128)(2,1)S(1)}, bf16[64,2304]{1,0:T(8,128)(2,1)S(1)}, u32[]{:S(2)}, u32[]{:S(2)}) %collective-permute-start.31) | collective-permute-done | bytes 294944 | tf_op jit(solution)/shard_map/ppermute | solution.py:101
  387.4 10.8 %collective-permute-done.30 = bf16[64,2304]{1,0:T(8,128)(2,1)S(1)} collective-permute-done((bf16[64,2304]{1,0:T(8,128)(2,1)S(1)}, bf16[64,2304]{1,0:T(8,128)(2,1)S(1)}, u32[]{:S(2)}, u32[]{:S(2)}) %collective-permute-start.30) | collective-permute-done | bytes 294944 | tf_op jit(solution)/shard_map/ppermute | solution.py:101
  403.1 8.8 %collective-permute-done.34 = bf16[64,2304]{1,0:T(8,128)(2,1)S(1)} collective-permute-done((bf16[64,2304]{1,0:T(8,128)(2,1)S(1)}, bf16[64,2304]{1,0:T(8,128)(2,1)S(1)}, u32[]{:S(2)}, u32[]{:S(2)}) %collective-permute-start.34) | collective-permute-done | bytes 294944 | tf_op jit(solution)/shard_map/ppermute | solution.py:101
  416.4 6.8 %collective-permute-done.35 = bf16[64,2304]{1,0:T(8,128)(2,1)S(1)} collective-permute-done((bf16[64,2304]{1,0:T(8,128)(2,1)S(1)}, bf16[64,2304]{1,0:T(8,128)(2,1)S(1)}, u32[]{:S(2)}, u32[]{:S(2)}) %collective-permute-start.35) | collective-permute-done | bytes 294944 | tf_op jit(solution)/shard_map/ppermute | solution.py:101
  427.8 9.6 %attend_backward.1 = (f32[512,256]{1,0:T(8,128)}, f32[2048,256]{1,0:T(8,128)}, bf16[2048,256]{1,0:T(8,128)(2,1)}) custom-call(s32[1]{0:T(128)} %bitcast.core_ref, bf16[512,256]{1,0:T(8,128)(2,1)} %copy-done.25, bf16[2048,256]{1,0:T(8,128)(2,1)} %copy-done.19, bf16[2048,256]{1,0:T(8,128)(2,1)} %copy-done.18, s32[512,1]{1,0:T(8,128)} %broadcast_select_fusion.2.spot_ref, ...), custom_call_target="tpu_custom_call" | custom-call | flops 115000000512 | tf_op jit(solution)/shard_map/attend_backward/pallas_call | solution.py:555
  448.8 6.5 %collective-permute-done.39 = bf16[512,256]{1,0:T(8,128)(2,1)} collective-permute-done((bf16[512,256]{1,0:T(8,128)(2,1)}, bf16[512,256]{1,0:T(8,128)(2,1)}, u32[]{:S(2)}, u32[]{:S(2)}) %collective-permute-start.39) | collective-permute-done | bytes 262176 | tf_op jit(solution)/shard_map/ppermute | solution.py:112
  458.7 6.7 %collective-permute-done.38 = bf16[512,256]{1,0:T(8,128)(2,1)S(1)} collective-permute-done((bf16[512,256]{1,0:T(8,128)(2,1)S(1)}, bf16[512,256]{1,0:T(8,128)(2,1)S(1)}, u32[]{:S(2)}, u32[]{:S(2)}) %collective-permute-start.38) | collective-permute-done | bytes 262176 | tf_op jit(solution)/shard_map/ppermute | solution.py:112
  472.7 6.9 %all-to-all-done.3.grad_ref = bf16[4,144,1152]{2,1,0:T(8,128)(2,1)S(1)} async-done(((bf16[4,144,1152]{2,1,0:T(8,128)(2,1)}), bf16[4,144,1152]{2,1,0:T(8,128)(2,1)S(1)}, u32[]{:S(2)}, u32[]{:S(2)}) %all-to-all-start.3) | async-done | bytes 1327136 | tf_op jit(solution)/shard_map/all_to_all | solution.py:140
  492.7 6.4 %copy.159 = bf16[2304,896]{1,0:T(8,128)(2,1)} copy(bf16[2304,896]{0,1:T(8,128)(2,1)} %pad_maximum_fusion) | data formatting | bytes 8257536 | tf_op jit(solution)/shard_map/concatenate | solution.py:827
  501.4 7.8 %collective-permute-done.43 = bf16[64,2304]{1,0:T(8,128)(2,1)S(1)} collective-permute-done((bf16[64,2304]{1,0:T(8,128)(2,1)S(1)}, bf16[64,2304]{1,0:T(8,128)(2,1)S(1)}, u32[]{:S(2)}, u32[]{:S(2)}) %collective-permute-start.43) | collective-permute-done | bytes 294944 | tf_op jit(solution)/shard_map/ppermute | solution.py:101
  511.8 9.2 %collective-permute-done.42 = bf16[64,2304]{1,0:T(8,128)(2,1)S(1)} collective-permute-done((bf16[64,2304]{1,0:T(8,128)(2,1)S(1)}, bf16[64,2304]{1,0:T(8,128)(2,1)S(1)}, u32[]{:S(2)}, u32[]{:S(2)}) %collective-permute-start.42) | collective-permute-done | bytes 294944 | tf_op jit(solution)/shard_map/ppermute | solution.py:101
  531.7 6.1 adam_shrink.1
  540.3 35.3 %reduce-scatter.6.cloned.1.call-done = bf16[4,144,896]{2,1,0:T(8,128)(2,1)} async-done(((bf16[4,576,896]{2,1,0:T(8,128)(2,1)}), bf16[4,144,896]{2,1,0:T(8,128)(2,1)}) %reduce-scatter.6.cloned.1.call-update) | async-done | bytes 1032208 | tf_op jit(solution)/shard_map/reduce_scatter | solution.py:180
  575.6 11.8 %all-to-all-done.4.grad_ref = bf16[4,144,2304]{2,1,0:T(8,128)(2,1)} async-done(((bf16[4,144,2304]{2,1,0:T(8,128)(2,1)}), bf16[4,144,2304]{2,1,0:T(8,128)(2,1)}, u32[]{:S(2)}, u32[]{:S(2)}) %all-to-all-start.4) | async-done | bytes 2654240 | tf_op jit(solution)/shard_map/all_to_all | solution.py:140
  596.2 17.1 %adam_expand.1 = (f32[144,2,4608]{2,1,0:T(2,128)}, f32[144,2,4608]{2,1,0:T(2,128)}, f32[144,2,4608]{2,1,0:T(2,128)}, f32[144,2,4608]{2,1,0:T(2,128)}) custom-call(bf16[4,144,2304]{2,1,0:T(8,128)(2,1)} %all-to-all-done.4.grad_ref, f32[144,2,4608]{2,1,0:T(2,128)S(1)} %copy-done.4, f32[144,2,4608]{2,1,0:T(2,128)S(1)} %copy-done.28, f32[144,2,4608]{2,1,0:T(2,128)} %refs_2_.1), custom_call_target="tpu_custom_call" | custom-call | flops 69000003584 | tf_op jit(solution)/shard_map/adam_expand/pallas_call | solution.py:312
  (420 shorter events, 267.2 us)
Async XLA Ops:
  14.1 46.4 %all-to-all-start = ((bf16[4,144,896]{2,1,0:T(8,128)(2,1)}), bf16[4,144,896]{2,1,0:T(8,128)(2,1)S(1)}, u32[]{:S(2)}, u32[]{:S(2)}) async-start(bf16[4,144,896]{2,1,0:T(8,128)(2,1)} %maximum_select_fusion.1), calls=%async_computation | async-start | bytes 2064384 | tf_op jit(solution)/shard_map/all_to_all | solution.py:140
  20.3 49.0 %all-gather.4.cloned.1.call-start = ((), (), s32[]{:S(2)}) async-start(), calls=%async_computation.9 | async-start | bytes 1474560 | tf_op jit(solution)/shard_map/all_gather | solution.py:706
  60.5 33.0 %all-to-all-start.1 = ((bf16[4,144,1152]{2,1,0:T(8,128)(2,1)}), bf16[4,144,1152]{2,1,0:T(8,128)(2,1)}, u32[]{:S(2)}, u32[]{:S(2)}) async-start(bf16[4,144,1152]{2,1,0:T(8,128)(2,1)} %get-tuple-element.68), calls=%async_computation.1 | async-start | bytes 2654208 | tf_op jit(solution)/shard_map/all_to_all | solution.py:140
  64.8 177.5 %all-gather.6.cloned.1.call-start = ((), (), s32[]{:S(2)}) async-start(), calls=%async_computation.10 | async-start | bytes 6635520 | tf_op jit(solution)/shard_map/all_gather | solution.py:175
  66.9 17.5 %collective-permute-start.2 = (bf16[4,144,640]{2,1,0:T(8,128)(2,1)}, bf16[4,144,640]{2,1,0:T(8,128)(2,1)S(1)}, u32[]{:S(2)}, u32[]{:S(2)}) collective-permute-start(bf16[4,144,640]{2,1,0:T(8,128)(2,1)} %slice.180), channel_id=1, source_target_pairs={{0,2},{1,5},{2,0},{3,7},{4,6},{5,1},{6,4},{7,3},{8,10},{9,13},{10,... | collective-permute-start | bytes 2211848 | tf_op jit(solution)/shard_map/ppermute | solution.py:112
  69.3 18.6 %collective-permute-start = (bf16[256,2304]{1,0:T(8,128)(2,1)}, bf16[256,2304]{1,0:T(8,128)(2,1)S(1)}, u32[]{:S(2)}, u32[]{:S(2)}) collective-permute-start(bf16[256,2304]{1,0:T(8,128)(2,1)} %all-gather.4.cloned.1.call-done), channel_id=1, source_target_pairs={{0,1},{1,0},{2,3},{3,2},{4,5},{5,4},{6,7},{7,6},{8,9},{9,8},{10,11... | collective-permute-start | bytes 3538952 | tf_op jit(solution)/shard_map/ppermute | solution.py:104
  69.4 17.6 %collective-permute-start.3 = (bf16[4,144,640]{2,1,0:T(8,128)(2,1)}, bf16[4,144,640]{2,1,0:T(8,128)(2,1)S(1)}, u32[]{:S(2)}, u32[]{:S(2)}) collective-permute-start(bf16[4,144,640]{2,1,0:T(8,128)(2,1)} %slice.180), channel_id=1, source_target_pairs={{0,4},{1,3},{2,6},{3,1},{4,0},{5,7},{6,2},{7,5},{8,12},{9,11},{10,... | collective-permute-start | bytes 2211848 | tf_op jit(solution)/shard_map/ppermute | solution.py:112
  84.4 16.0 %collective-permute-start.4 = (bf16[4,144,640]{2,1,0:T(8,128)(2,1)S(1)}, bf16[4,144,640]{2,1,0:T(8,128)(2,1)}, u32[]{:S(2)}, u32[]{:S(2)}) collective-permute-start(bf16[4,144,640]{2,1,0:T(8,128)(2,1)S(1)} %collective-permute-done.2), channel_id=1, source_target_pairs={{0,4},{1,3},{2,6},{3,1},{4,0},{5,7},{6,2},{7,5},{8,12},{9,11},{10,... | collective-permute-start | bytes 2211848 | tf_op jit(solution)/shard_map/ppermute | solution.py:112
  96.6 63.3 %all-to-all-start.2 = ((bf16[4,144,2304]{2,1,0:T(8,128)(2,1)}), bf16[4,144,2304]{2,1,0:T(8,128)(2,1)S(1)}, u32[]{:S(2)}, u32[]{:S(2)}) async-start(bf16[4,144,2304]{2,1,0:T(8,128)(2,1)} %pad_maximum_fusion.1), calls=%async_computation.2 | async-start | bytes 5308416 | tf_op jit(solution)/shard_map/all_to_all | solution.py:140
  100.3 169.3 %all-gather.8.cloned.1.call-start = ((), (), s32[]{:S(2)}) async-start(), calls=%async_computation.11 | async-start | bytes 13271040 | tf_op jit(solution)/shard_map/all_gather | solution.py:175
  118.0 43.5 %collective-permute-start.6 = (bf16[512,256]{1,0:T(8,128)(2,1)}, bf16[512,256]{1,0:T(8,128)(2,1)}, u32[]{:S(2)}, u32[]{:S(2)}) collective-permute-start(bf16[512,256]{1,0:T(8,128)(2,1)} %get-tuple-element.164), channel_id=1, source_target_pairs={{0,4},{1,3},{2,6},{3,1},{4,0},{5,7},{6,2},{7,5},{8,12},{9,11},{10,... | collective-permute-start | bytes 786440 | tf_op jit(solution)/shard_map/ppermute | solution.py:112
  124.3 38.9 %collective-permute-start.7 = (bf16[512,256]{1,0:T(8,128)(2,1)}, bf16[512,256]{1,0:T(8,128)(2,1)}, u32[]{:S(2)}, u32[]{:S(2)}) collective-permute-start(bf16[512,256]{1,0:T(8,128)(2,1)} %collective-permute-done.5), channel_id=1, source_target_pairs={{0,4},{1,3},{2,6},{3,1},{4,0},{5,7},{6,2},{7,5},{8,12},{9,11},{10,... | collective-permute-start | bytes 786440 | tf_op jit(solution)/shard_map/ppermute | solution.py:112
  161.4 282.6 %reduce-scatter.4.cloned.1.call-start = ((), (), s32[]{:S(2)}) async-start(), calls=%async_computation.12 | async-start | bytes 6635520 | tf_op jit(solution)/shard_map/reduce_scatter | solution.py:180
  166.3 17.1 %collective-permute-start.8 = (bf16[2048,256]{1,0:T(8,128)(2,1)}, bf16[2048,256]{1,0:T(8,128)(2,1)S(1)}, u32[]{:S(2)}, u32[]{:S(2)}) collective-permute-start(bf16[2048,256]{1,0:T(8,128)(2,1)} %bitcast.291), channel_id=1, source_target_pairs={{0,1},{1,0},{2,3},{3,2},{4,5},{5,4},{6,7},{7,6},{8,9},{9,8},{10,11... | collective-permute-start | bytes 3145736 | tf_op jit(solution)/shard_map/ppermute | solution.py:104
  170.2 13.2 %collective-permute-start.11 = (bf16[4,144,256]{2,1,0:T(8,128)(2,1)S(1)}, bf16[4,144,256]{2,1,0:T(8,128)(2,1)S(1)}, u32[]{:S(2)}, u32[]{:S(2)}) collective-permute-start(bf16[4,144,256]{2,1,0:T(8,128)(2,1)S(1)} %collective-permute-done.9), channel_id=1, source_target_pairs={{0,4},{1,3},{2,6},{3,1},{4,0},{5,7},{6,2},{7,5},{8,12},{9,11},{10,... | collective-permute-start | bytes 884744 | tf_op jit(solution)/shard_map/ppermute | solution.py:112
  193.8 21.9 %collective-permute-start.13 = (bf16[64,2304]{1,0:T(8,128)(2,1)S(1)}, bf16[64,2304]{1,0:T(8,128)(2,1)S(1)}, u32[]{:S(2)}, u32[]{:S(2)}) collective-permute-start(bf16[64,2304]{1,0:T(8,128)(2,1)S(1)} %get-tuple-element.174), channel_id=1, source_target_pairs={{0,8},{8,0},{16,24},{24,16},{1,9},{9,1},{17,25},{25,17},{2,10},{10... | collective-permute-start | bytes 884744 | tf_op jit(solution)/shard_map/ppermute | solution.py:101
  219.8 15.1 %collective-permute-start.16 = (bf16[64,2304]{1,0:T(8,128)(2,1)S(1)}, bf16[64,2304]{1,0:T(8,128)(2,1)S(1)}, u32[]{:S(2)}, u32[]{:S(2)}) collective-permute-start(bf16[64,2304]{1,0:T(8,128)(2,1)S(1)} %get-tuple-element.158), channel_id=1, source_target_pairs={{0,8},{8,0},{16,24},{24,16},{1,9},{9,1},{17,25},{25,17},{2,10},{10... | collective-permute-start | bytes 884744 | tf_op jit(solution)/shard_map/ppermute | solution.py:101
  229.4 12.8 %collective-permute-start.18 = (bf16[64,2304]{1,0:T(8,128)(2,1)S(1)}, bf16[64,2304]{1,0:T(8,128)(2,1)S(1)}, u32[]{:S(2)}, u32[]{:S(2)}) collective-permute-start(bf16[64,2304]{1,0:T(8,128)(2,1)S(1)} %collective-permute-done.17), channel_id=1, source_target_pairs={{0,8},{8,0},{16,24},{24,16},{1,9},{9,1},{17,25},{25,17},{2,10},{10... | collective-permute-start | bytes 884744 | tf_op jit(solution)/shard_map/ppermute | solution.py:101
  288.8 13.9 %collective-permute-start.21 = (bf16[64,2304]{1,0:T(8,128)(2,1)S(1)}, bf16[64,2304]{1,0:T(8,128)(2,1)S(1)}, u32[]{:S(2)}, u32[]{:S(2)}) collective-permute-start(bf16[64,2304]{1,0:T(8,128)(2,1)S(1)} %get-tuple-element.172), channel_id=1, source_target_pairs={{0,8},{8,0},{16,24},{24,16},{1,9},{9,1},{17,25},{25,17},{2,10},{10... | collective-permute-start | bytes 884744 | tf_op jit(solution)/shard_map/ppermute | solution.py:101
  297.3 13.7 %collective-permute-start.23 = (bf16[64,2304]{1,0:T(8,128)(2,1)S(1)}, bf16[64,2304]{1,0:T(8,128)(2,1)S(1)}, u32[]{:S(2)}, u32[]{:S(2)}) collective-permute-start(bf16[64,2304]{1,0:T(8,128)(2,1)S(1)} %fusion.43), channel_id=1, source_target_pairs={{0,24},{8,16},{16,8},{24,0},{1,25},{9,17},{17,9},{25,1},{2,26},{10... | collective-permute-start | bytes 884744 | tf_op jit(solution)/shard_map/ppermute | solution.py:101
  314.6 15.0 %collective-permute-start.25 = (bf16[64,2304]{1,0:T(8,128)(2,1)S(1)}, bf16[64,2304]{1,0:T(8,128)(2,1)S(1)}, u32[]{:S(2)}, u32[]{:S(2)}) collective-permute-start(bf16[64,2304]{1,0:T(8,128)(2,1)S(1)} %get-tuple-element.154), channel_id=1, source_target_pairs={{0,8},{8,0},{16,24},{24,16},{1,9},{9,1},{17,25},{25,17},{2,10},{10... | collective-permute-start | bytes 884744 | tf_op jit(solution)/shard_map/ppermute | solution.py:101
  343.1 178.6 %reduce-scatter.8.cloned.1.call-start = ((), (), s32[]{:S(2)}) async-start(), calls=%async_computation.14 | async-start | bytes 13271040 | tf_op jit(solution)/shard_map/reduce_scatter | solution.py:180
  376.6 21.7 %collective-permute-start.30 = (bf16[64,2304]{1,0:T(8,128)(2,1)S(1)}, bf16[64,2304]{1,0:T(8,128)(2,1)S(1)}, u32[]{:S(2)}, u32[]{:S(2)}) collective-permute-start(bf16[64,2304]{1,0:T(8,128)(2,1)S(1)} %get-tuple-element.168), channel_id=1, source_target_pairs={{0,8},{8,0},{16,24},{24,16},{1,9},{9,1},{17,25},{25,17},{2,10},{10... | collective-permute-start | bytes 884744 | tf_op jit(solution)/shard_map/ppermute | solution.py:101
  402.4 14.0 %collective-permute-start.33 = (bf16[64,2304]{1,0:T(8,128)(2,1)S(1)}, bf16[64,2304]{1,0:T(8,128)(2,1)S(1)}, u32[]{:S(2)}, u32[]{:S(2)}) collective-permute-start(bf16[64,2304]{1,0:T(8,128)(2,1)S(1)} %get-tuple-element.150), channel_id=1, source_target_pairs={{0,8},{8,0},{16,24},{24,16},{1,9},{9,1},{17,25},{25,17},{2,10},{10... | collective-permute-start | bytes 884744 | tf_op jit(solution)/shard_map/ppermute | solution.py:101
  444.1 35.5 %all-to-all-start.3 = ((bf16[4,144,1152]{2,1,0:T(8,128)(2,1)}), bf16[4,144,1152]{2,1,0:T(8,128)(2,1)S(1)}, u32[]{:S(2)}, u32[]{:S(2)}) async-start(bf16[4,144,1152]{2,1,0:T(8,128)(2,1)} %reduce-scatter.4.cloned.1.call-done), calls=%async_computation.4 | async-start | bytes 2654208 | tf_op jit(solution)/shard_map/all_to_all | solution.py:140
  447.6 127.9 %reduce-scatter.6.cloned.1.call-start = ((), (), s32[]{:S(2)}) async-start(), calls=%async_computation.13 | async-start | bytes 5160960 | tf_op jit(solution)/shard_map/reduce_scatter | solution.py:180
  447.7 17.7 %collective-permute-start.38 = (bf16[512,256]{1,0:T(8,128)(2,1)S(1)}, bf16[512,256]{1,0:T(8,128)(2,1)S(1)}, u32[]{:S(2)}, u32[]{:S(2)}) collective-permute-start(bf16[512,256]{1,0:T(8,128)(2,1)S(1)} %get-tuple-element.182), channel_id=1, source_target_pairs={{0,4},{1,3},{2,6},{3,1},{4,0},{5,7},{6,2},{7,5},{8,12},{9,11},{10,... | collective-permute-start | bytes 786440 | tf_op jit(solution)/shard_map/ppermute | solution.py:112
  456.4 13.0 %collective-permute-start.40 = (bf16[512,256]{1,0:T(8,128)(2,1)S(1)}, bf16[512,256]{1,0:T(8,128)(2,1)S(1)}, u32[]{:S(2)}, u32[]{:S(2)}) collective-permute-start(bf16[512,256]{1,0:T(8,128)(2,1)S(1)} %fusion.53), channel_id=1, source_target_pairs={{0,2},{1,5},{2,0},{3,7},{4,6},{5,1},{6,4},{7,3},{8,10},{9,13},{10,... | collective-permute-start | bytes 786440 | tf_op jit(solution)/shard_map/ppermute | solution.py:112
  500.2 20.8 %collective-permute-start.42 = (bf16[64,2304]{1,0:T(8,128)(2,1)S(1)}, bf16[64,2304]{1,0:T(8,128)(2,1)S(1)}, u32[]{:S(2)}, u32[]{:S(2)}) collective-permute-start(bf16[64,2304]{1,0:T(8,128)(2,1)S(1)} %get-tuple-element.166), channel_id=1, source_target_pairs={{0,8},{8,0},{16,24},{24,16},{1,9},{9,1},{17,25},{25,17},{2,10},{10... | collective-permute-start | bytes 884744 | tf_op jit(solution)/shard_map/ppermute | solution.py:101
  521.5 16.3 %collective-permute-start.45 = (f32[64,2304]{1,0:T(8,128)S(1)}, f32[64,2304]{1,0:T(8,128)}, u32[]{:S(2)}, u32[]{:S(2)}) collective-permute-start(f32[64,2304]{1,0:T(8,128)S(1)} %last_grad.1), channel_id=1, source_target_pairs={{0,1},{1,0},{2,3},{3,2},{4,5},{5,4},{6,7},{7,6},{8,9},{9,8},{10,11... | collective-permute-start | bytes 1769480 | tf_op jit(solution)/shard_map/ppermute | solution.py:104
  521.7 65.7 %all-to-all-start.4 = ((bf16[4,144,2304]{2,1,0:T(8,128)(2,1)}), bf16[4,144,2304]{2,1,0:T(8,128)(2,1)}, u32[]{:S(2)}, u32[]{:S(2)}) async-start(bf16[4,144,2304]{2,1,0:T(8,128)(2,1)} %reduce-scatter.8.cloned.1.call-done), calls=%async_computation.7 | async-start | bytes 5308416 | tf_op jit(solution)/shard_map/all_to_all | solution.py:140
  587.4 29.2 %all-to-all-start.5 = ((bf16[4,144,896]{2,1,0:T(8,128)(2,1)}), bf16[4,144,896]{2,1,0:T(8,128)(2,1)S(1)}, u32[]{:S(2)}, u32[]{:S(2)}) async-start(bf16[4,144,896]{2,1,0:T(8,128)(2,1)} %reduce-scatter.6.cloned.1.call-done), calls=%async_computation.8 | async-start | bytes 2064384 | tf_op jit(solution)/shard_map/all_to_all | solution.py:140
  (113 other events, 1019.8 us)
Sparse Core Ops, SparseCore 0:
  23.3 45.9 all-gather.3
Sparse Core Ops, SparseCore 1:
  93.6 64.4 all-gather.5
  161.5 108.1 all-gather.7
  343.2 60.6 reduce-scatter.3
  406.9 112.9 reduce-scatter.7
  523.5 52.0 reduce-scatter.5

commit v2 on v1

--- a/solution.py
+++ b/solution.py
@@ -200,24 +200,6 @@
     return 16 if local_width % 16 == 0 else local_width
 
 
-def attend_rows(array):
-    rows, groups, slots, width = array.shape
-    tiles = width // TILE
-    shaped = array.reshape(rows, groups, slots, tiles, TILE).transpose(0, 1, 3, 2, 4)
-    return shaped.reshape(-1, TILE)
-
-
-def attend_from_rows(array, shape):
-    rows, groups, slots, width = shape
-    tiles = width // TILE
-    shaped = array.reshape(rows, groups, tiles, slots, TILE).transpose(0, 1, 3, 2, 4)
-    return shaped.reshape(shape)
-
-
-def row_block(rows, height):
-    return pl.BlockSpec((rows * height, TILE), lambda i, *_: (i, 0))
-
-
 def pack_expand(weight):
     local_width, _, width = weight.shape
     rows = rows_per_step(local_width)
@@ -266,20 +248,18 @@
 def pack_attend(weight, gains, core):
     local_width, groups, slots, width = weight.shape
     rows = rows_per_step(local_width)
-    tiles = width // TILE
-    height = groups * slots * tiles
     columns = 2 * width + TILE
 
     def kernel(core_ref, in_ref, gains_ref, own_ref, other_ref):
-        for out_ref, member in ((own_ref, core_ref[0]), (other_ref, 1 - core_ref[0])):
-            for group in range(groups):
-                for pair in range(2):
-                    for tile in range(tiles):
-                        first = (group * tiles + tile) * slots + 2 * pair
-                        chosen = pl.ds(first + member, rows, stride=height)
-                        column = (pair * tiles + tile) * TILE
-                        out_ref[group, :, column : column + TILE] = in_ref[chosen, :].astype(BF16)
-                out_ref[group, :, 2 * width :] = gains_ref[...].astype(BF16)
+        first_core = core_ref[0] == 0
+        for group in range(groups):
+            for pair in range(2):
+                first, second = in_ref[:, group, 2 * pair, :], in_ref[:, group, 2 * pair + 1, :]
+                place = slice(pair * width, (pair + 1) * width)
+                own_ref[group, :, place] = jnp.where(first_core, first, second).astype(BF16)
+                other_ref[group, :, place] = jnp.where(first_core, second, first).astype(BF16)
+            own_ref[group, :, 2 * width :] = gains_ref[...].astype(BF16)
+            other_ref[group, :, 2 * width :] = gains_ref[...].astype(BF16)
 
     pack = jax.ShapeDtypeStruct((groups, local_width, columns), BF16)
     gain_columns = jnp.pad(gains.T, ((0, 0), (0, TILE - gains.shape[0])))
@@ -290,7 +270,7 @@
             num_scalar_prefetch=1,
             grid=(local_width // rows,),
             in_specs=[
-                row_block(rows, height),
+                pl.BlockSpec((rows, groups, slots, width), lambda i, *_: (i, 0, 0, 0)),
                 pl.BlockSpec((rows, TILE), lambda i, *_: (i, 0)),
             ],
             out_specs=[pl.BlockSpec((groups, rows, columns), lambda i, *_: (0, i, 0))] * 2,
@@ -298,7 +278,7 @@
         compiler_params=pltpu.CompilerParams(vmem_limit_bytes=32 << 20),
         cost_estimate=pl.CostEstimate(flops=0, bytes_accessed=6 * weight.size, transcendentals=0),
         name="pack_attend",
-    )(core.reshape(1), attend_rows(weight), gain_columns)
+    )(core.reshape(1), weight, gain_columns)
 
 
 def adam_tile(grad, chosen, in_refs, out_refs):
@@ -350,36 +330,32 @@
 
 
 def adam_attend(weight, moment, square, own, other, core):
-    shape = weight.shape
-    local_width, groups, slots, width = shape
+    local_width, groups, slots, width = weight.shape
     rows = rows_per_step(local_width)
-    tiles = width // TILE
-    height = groups * slots * tiles
 
     def kernel(core_ref, own_ref, other_ref, *refs):
-        in_refs, out_refs = refs[:3], refs[3:]
-        for grad_ref, member in ((own_ref, core_ref[0]), (other_ref, 1 - core_ref[0])):
-            for group in range(groups):
-                for pair in range(2):
-                    for tile in range(tiles):
-                        first = (group * tiles + tile) * slots + 2 * pair
-                        chosen = (pl.ds(first + member, rows, stride=height), slice(None))
-                        column = (pair * tiles + tile) * TILE
-                        grad = grad_ref[group, :, column : column + TILE].astype(F32)
-                        adam_tile(grad, chosen, in_refs, out_refs)
-
-    results = adam_call(
+        first_core = core_ref[0] == 0
+        for group in range(groups):
+            for pair in range(2):
+                place = slice(pair * width, (pair + 1) * width)
+                kept = own_ref[group, :, place].astype(F32)
+                came = other_ref[group, :, place].astype(F32)
+                for member in range(2):
+                    grad = jnp.where(first_core == (member == 0), kept, came)
+                    chosen = (slice(None), group, 2 * pair + member, slice(None))
+                    adam_tile(grad, chosen, refs[:3], refs[3:])
+
+    return adam_call(
         kernel,
         (core.reshape(1),),
         [own, other],
         [pl.BlockSpec((groups, rows, own.shape[-1]), lambda i, *_: (0, i, 0))] * 2,
-        [attend_rows(a) for a in (weight, moment, square)],
-        row_block(rows, height),
+        [weight, moment, square],
+        pl.BlockSpec((rows, groups, slots, width), lambda i, *_: (i, 0, 0, 0)),
         local_width // rows,
         "adam_attend",
         10,
     )
-    return [attend_from_rows(a, shape) for a in results]
 
 
 def adam_shrink(weight, moment, square, grad):

time: 643 us -> 645 us (level)
  no operation moved by 1% of the time
where the time goes in v2:
time: 645 us; the launch traced here: 637 us
  waiting for transfers between devices  325 us (50%)
  starting transfers between devices  84.6 us (13%)
  Pallas kernels  65.6 us (10%)
  local copies, waits for them, and re-layouts  62.5 us (10%)
  matrix products  43.2 us (7%)
  other arithmetic  37.7 us (6%)
  between operations  17.5 us (3%)
    ppermute x21, waiting for transfers between devices, along(): return lax.ppermute(value, 'line', pairs)  118 us
    all_to_all x6, waiting for transfers between devices, line_swap(): lax.all_to_all(blocks, 'line', split_axis=0, concat_axis=0, tiled=True)  88.6 us
    ppermute x12, waiting for transfers between devices, within(): return lax.ppermute(value, ('place', 'head'), pairs)  40.2 us
    ppermute x21, starting transfers between devices, along(): return lax.ppermute(value, 'line', pairs)  37.6 us
    unnamed x169, local copies, waits for them, and re-layouts  37.3 us
    reduce_scatter x3, waiting for transfers between devices, bulk_sum(): return lax.psum_scatter(shaped, 'place', scatter_dimension=1, tiled=True)  35.3 us
    pallas_call x3, Pallas kernels, adam_call(): pl.pallas_call(kernel, out_shape=[jax.ShapeDtypeStruct(states[0].shape, F...  29.3 us
    all_to_all x6, starting transfers between devices, line_swap(): lax.all_to_all(blocks, 'line', split_axis=0, concat_axis=0, tiled=True)  26.4 us
  transfers between devices with their start and end apart: 61, of which 43 were waited for; matrix products, arithmetic and copies ran while one was open for 15% of the time, Pallas kernels for 8%

profile of v2, /device:TPU:0, one launch (start us, length us, event | category | flops | bytes accessed | tf_op | source)
XLA Modules:
  0.0 636.6 jit_solution(10022811877138778999)
XLA Ops:
  15.3 6.2 all-to-all-start
  25.2 6.2 pack_expand.1
  32.6 29.1 %all-to-all-done = bf16[4,144,896]{2,1,0:T(8,128)(2,1)S(1)} async-done(((bf16[4,144,896]{2,1,0:T(8,128)(2,1)}), bf16[4,144,896]{2,1,0:T(8,128)(2,1)S(1)}, u32[]{:S(2)}, u32[]{:S(2)}) %all-to-all-start) | async-done | bytes 1032224 | tf_op jit(solution)/shard_map/all_to_all | solution.py:140
  78.9 6.6 %collective-permute-done.2 = bf16[4,144,640]{2,1,0:T(8,128)(2,1)S(1)} collective-permute-done((bf16[4,144,640]{2,1,0:T(8,128)(2,1)}, bf16[4,144,640]{2,1,0:T(8,128)(2,1)S(1)}, u32[]{:S(2)}, u32[]{:S(2)}) %collective-permute-start.2) | collective-permute-done | bytes 737312 | tf_op jit(solution)/shard_map/ppermute | solution.py:112
  129.1 32.0 %all-to-all-done.2 = bf16[4,144,2304]{2,1,0:T(8,128)(2,1)S(1)} async-done(((bf16[4,144,2304]{2,1,0:T(8,128)(2,1)}), bf16[4,144,2304]{2,1,0:T(8,128)(2,1)S(1)}, u32[]{:S(2)}, u32[]{:S(2)}) %all-to-all-start.2) | async-done | bytes 2654240 | tf_op jit(solution)/shard_map/all_to_all | solution.py:140
  175.1 9.4 %collective-permute-done.11 = bf16[4,144,256]{2,1,0:T(8,128)(2,1)S(1)} collective-permute-done((bf16[4,144,256]{2,1,0:T(8,128)(2,1)S(1)}, bf16[4,144,256]{2,1,0:T(8,128)(2,1)S(1)}, u32[]{:S(2)}, u32[]{:S(2)}) %collective-permute-start.11) | collective-permute-done | bytes 294944 | tf_op jit(solution)/shard_map/ppermute | solution.py:112
  197.0 7.8 %collective-permute-done.14 = bf16[64,2304]{1,0:T(8,128)(2,1)S(1)} collective-permute-done((bf16[64,2304]{1,0:T(8,128)(2,1)S(1)}, bf16[64,2304]{1,0:T(8,128)(2,1)S(1)}, u32[]{:S(2)}, u32[]{:S(2)}) %collective-permute-start.14) | collective-permute-done | bytes 294944 | tf_op jit(solution)/shard_map/ppermute | solution.py:101
  206.0 10.9 %collective-permute-done.13 = bf16[64,2304]{1,0:T(8,128)(2,1)S(1)} collective-permute-done((bf16[64,2304]{1,0:T(8,128)(2,1)S(1)}, bf16[64,2304]{1,0:T(8,128)(2,1)S(1)}, u32[]{:S(2)}, u32[]{:S(2)}) %collective-permute-start.13) | collective-permute-done | bytes 294944 | tf_op jit(solution)/shard_map/ppermute | solution.py:101
  223.1 7.5 %collective-permute-done.17 = bf16[64,2304]{1,0:T(8,128)(2,1)S(1)} collective-permute-done((bf16[64,2304]{1,0:T(8,128)(2,1)S(1)}, bf16[64,2304]{1,0:T(8,128)(2,1)S(1)}, u32[]{:S(2)}, u32[]{:S(2)}) %collective-permute-start.17) | collective-permute-done | bytes 294944 | tf_op jit(solution)/shard_map/ppermute | solution.py:101
  236.1 7.3 %collective-permute-done.18 = bf16[64,2304]{1,0:T(8,128)(2,1)S(1)} collective-permute-done((bf16[64,2304]{1,0:T(8,128)(2,1)S(1)}, bf16[64,2304]{1,0:T(8,128)(2,1)S(1)}, u32[]{:S(2)}, u32[]{:S(2)}) %collective-permute-start.18) | collective-permute-done | bytes 294944 | tf_op jit(solution)/shard_map/ppermute | solution.py:101
  247.9 23.0 %all-gather.8.cloned.1.call-done = bf16[4,576,2304]{2,1,0:T(8,128)(2,1)} async-done(((bf16[4,144,2304]{2,1,0:T(8,128)(2,1)}), bf16[4,576,2304]{2,1,0:T(8,128)(2,1)}) %all-gather.8.cloned.1.call-update) | async-done | bytes 10616848 | tf_op jit(solution)/shard_map/all_gather | solution.py:175
  275.0 8.5 %gate_and_up.1 = (f32[512,1152]{1,0:T(8,128)S(1)}, f32[512,1152]{1,0:T(8,128)S(1)}, bf16[512,1152]{1,0:T(8,128)(2,1)S(1)}) custom-call(bf16[512,2304]{1,0:T(8,128)(2,1)S(1)} %copy-done.21, bf16[2304,1152]{1,0:T(8,128)(2,1)S(1)} %bitcast.223, bf16[2304,2304]{1,0:T(8,128)(2,1)} %bitcast.210), custom_call_target="tpu_custom_call" | custom-call | flops 5435817984 | bytes 10616832 | tf_op jit(solution)/shard_map/gate_and_up/pallas_call | solution.py:597
  290.5 7.8 %collective-permute-done.22 = bf16[64,2304]{1,0:T(8,128)(2,1)S(1)} collective-permute-done((bf16[64,2304]{1,0:T(8,128)(2,1)S(1)}, bf16[64,2304]{1,0:T(8,128)(2,1)S(1)}, u32[]{:S(2)}, u32[]{:S(2)}) %collective-permute-start.22) | collective-permute-done | bytes 294944 | tf_op jit(solution)/shard_map/ppermute | solution.py:101
  303.9 8.3 %collective-permute-done.23 = bf16[64,2304]{1,0:T(8,128)(2,1)S(1)} collective-permute-done((bf16[64,2304]{1,0:T(8,128)(2,1)S(1)}, bf16[64,2304]{1,0:T(8,128)(2,1)S(1)}, u32[]{:S(2)}, u32[]{:S(2)}) %collective-permute-start.23) | collective-permute-done | bytes 294944 | tf_op jit(solution)/shard_map/ppermute | solution.py:101
  319.2 6.9 %collective-permute-done.26 = bf16[64,2304]{1,0:T(8,128)(2,1)S(1)} collective-permute-done((bf16[64,2304]{1,0:T(8,128)(2,1)S(1)}, bf16[64,2304]{1,0:T(8,128)(2,1)S(1)}, u32[]{:S(2)}, u32[]{:S(2)}) %collective-permute-start.26) | collective-permute-done | bytes 294944 | tf_op jit(solution)/shard_map/ppermute | solution.py:101
  351.5 6.4 %gate_and_up_back.1 = bf16[512,2304]{1,0:T(8,128)(2,1)S(1)} custom-call(bf16[512,2304]{1,0:T(8,128)(2,1)S(1)} %pad_maximum_fusion.3.feed_ref, f32[512,1152]{1,0:T(8,128)S(1)} %get-tuple-element.83.gate_ref, f32[512,1152]{1,0:T(8,128)S(1)} %copy-done.8, bf16[2304,2304]{1,0:T(8,128)(2,1)S(1)} %bitcast.213), custom_call_target="tpu_custom_call" | custom-call | flops 2717908992 | bytes 5308416 | tf_op jit(solution)/shard_map/gate_and_up_back/pallas_call | solution.py:631
  358.0 8.3 %convolution_convert_fusion = bf16[2304,2304]{1,0:T(8,128)(2,1)} fusion(bf16[512,2304]{1,0:T(8,128)(2,1)S(1)} %copy-done.22, bf16[512,2304]{1,0:T(8,128)(2,1)S(1)} %gate_and_up_back.1), kind=kOutput, calls=%fused_computation | convolution fusion | flops 5441126400 | bytes 15335424 | tf_op jit(solution)/shard_map/dot_general | solution.py:567
  379.7 7.8 %collective-permute-done.31 = bf16[64,2304]{1,0:T(8,128)(2,1)S(1)} collective-permute-done((bf16[64,2304]{1,0:T(8,128)(2,1)S(1)}, bf16[64,2304]{1,0:T(8,128)(2,1)S(1)}, u32[]{:S(2)}, u32[]{:S(2)}) %collective-permute-start.31) | collective-permute-done | bytes 294944 | tf_op jit(solution)/shard_map/ppermute | solution.py:101
  388.6 10.8 %collective-permute-done.30 = bf16[64,2304]{1,0:T(8,128)(2,1)S(1)} collective-permute-done((bf16[64,2304]{1,0:T(8,128)(2,1)S(1)}, bf16[64,2304]{1,0:T(8,128)(2,1)S(1)}, u32[]{:S(2)}, u32[]{:S(2)}) %collective-permute-start.30) | collective-permute-done | bytes 294944 | tf_op jit(solution)/shard_map/ppermute | solution.py:101
  404.2 8.9 %collective-permute-done.34 = bf16[64,2304]{1,0:T(8,128)(2,1)S(1)} collective-permute-done((bf16[64,2304]{1,0:T(8,128)(2,1)S(1)}, bf16[64,2304]{1,0:T(8,128)(2,1)S(1)}, u32[]{:S(2)}, u32[]{:S(2)}) %collective-permute-start.34) | collective-permute-done | bytes 294944 | tf_op jit(solution)/shard_map/ppermute | solution.py:101
  417.5 6.7 %collective-permute-done.35 = bf16[64,2304]{1,0:T(8,128)(2,1)S(1)} collective-permute-done((bf16[64,2304]{1,0:T(8,128)(2,1)S(1)}, bf16[64,2304]{1,0:T(8,128)(2,1)S(1)}, u32[]{:S(2)}, u32[]{:S(2)}) %collective-permute-start.35) | collective-permute-done | bytes 294944 | tf_op jit(solution)/shard_map/ppermute | solution.py:101
  428.8 9.6 %attend_backward.1 = (f32[512,256]{1,0:T(8,128)}, f32[2048,256]{1,0:T(8,128)}, bf16[2048,256]{1,0:T(8,128)(2,1)}) custom-call(s32[1]{0:T(128)} %bitcast.core_ref, bf16[512,256]{1,0:T(8,128)(2,1)} %copy-done.25, bf16[2048,256]{1,0:T(8,128)(2,1)} %copy-done.19, bf16[2048,256]{1,0:T(8,128)(2,1)} %copy-done.18, s32[512,1]{1,0:T(8,128)} %broadcast_select_fusion.2.spot_ref, ...), custom_call_target="tpu_custom_call" | custom-call | flops 115000000512 | tf_op jit(solution)/shard_map/attend_backward/pallas_call | solution.py:531
  449.9 6.5 %collective-permute-done.39 = bf16[512,256]{1,0:T(8,128)(2,1)} collective-permute-done((bf16[512,256]{1,0:T(8,128)(2,1)}, bf16[512,256]{1,0:T(8,128)(2,1)}, u32[]{:S(2)}, u32[]{:S(2)}) %collective-permute-start.39) | collective-permute-done | bytes 262176 | tf_op jit(solution)/shard_map/ppermute | solution.py:112
  459.8 6.6 %collective-permute-done.38 = bf16[512,256]{1,0:T(8,128)(2,1)S(1)} collective-permute-done((bf16[512,256]{1,0:T(8,128)(2,1)S(1)}, bf16[512,256]{1,0:T(8,128)(2,1)S(1)}, u32[]{:S(2)}, u32[]{:S(2)}) %collective-permute-start.38) | collective-permute-done | bytes 262176 | tf_op jit(solution)/shard_map/ppermute | solution.py:112
  473.8 7.0 %all-to-all-done.3.grad_ref = bf16[4,144,1152]{2,1,0:T(8,128)(2,1)S(1)} async-done(((bf16[4,144,1152]{2,1,0:T(8,128)(2,1)}), bf16[4,144,1152]{2,1,0:T(8,128)(2,1)S(1)}, u32[]{:S(2)}, u32[]{:S(2)}) %all-to-all-start.3) | async-done | bytes 1327136 | tf_op jit(solution)/shard_map/all_to_all | solution.py:140
  493.9 6.4 %copy.130 = bf16[2304,896]{1,0:T(8,128)(2,1)} copy(bf16[2304,896]{0,1:T(8,128)(2,1)} %pad_maximum_fusion) | data formatting | bytes 8257536 | tf_op jit(solution)/shard_map/concatenate | solution.py:803
  502.5 7.8 %collective-permute-done.43 = bf16[64,2304]{1,0:T(8,128)(2,1)S(1)} collective-permute-done((bf16[64,2304]{1,0:T(8,128)(2,1)S(1)}, bf16[64,2304]{1,0:T(8,128)(2,1)S(1)}, u32[]{:S(2)}, u32[]{:S(2)}) %collective-permute-start.43) | collective-permute-done | bytes 294944 | tf_op jit(solution)/shard_map/ppermute | solution.py:101
  512.9 9.2 %collective-permute-done.42 = bf16[64,2304]{1,0:T(8,128)(2,1)S(1)} collective-permute-done((bf16[64,2304]{1,0:T(8,128)(2,1)S(1)}, bf16[64,2304]{1,0:T(8,128)(2,1)S(1)}, u32[]{:S(2)}, u32[]{:S(2)}) %collective-permute-start.42) | collective-permute-done | bytes 294944 | tf_op jit(solution)/shard_map/ppermute | solution.py:101
  532.9 6.1 adam_shrink.1
  541.4 35.3 %reduce-scatter.6.cloned.1.call-done = bf16[4,144,896]{2,1,0:T(8,128)(2,1)} async-done(((bf16[4,576,896]{2,1,0:T(8,128)(2,1)}), bf16[4,144,896]{2,1,0:T(8,128)(2,1)}) %reduce-scatter.6.cloned.1.call-update) | async-done | bytes 1032208 | tf_op jit(solution)/shard_map/reduce_scatter | solution.py:180
  576.7 11.8 %all-to-all-done.4.grad_ref = bf16[4,144,2304]{2,1,0:T(8,128)(2,1)} async-done(((bf16[4,144,2304]{2,1,0:T(8,128)(2,1)}), bf16[4,144,2304]{2,1,0:T(8,128)(2,1)}, u32[]{:S(2)}, u32[]{:S(2)}) %all-to-all-start.4) | async-done | bytes 2654240 | tf_op jit(solution)/shard_map/all_to_all | solution.py:140
  597.4 17.1 %adam_expand.1 = (f32[144,2,4608]{2,1,0:T(2,128)}, f32[144,2,4608]{2,1,0:T(2,128)}, f32[144,2,4608]{2,1,0:T(2,128)}, f32[144,2,4608]{2,1,0:T(2,128)}) custom-call(bf16[4,144,2304]{2,1,0:T(8,128)(2,1)} %all-to-all-done.4.grad_ref, f32[144,2,4608]{2,1,0:T(2,128)S(1)} %copy-done.4, f32[144,2,4608]{2,1,0:T(2,128)S(1)} %copy-done.28, f32[144,2,4608]{2,1,0:T(2,128)} %refs_2_.3), custom_call_target="tpu_custom_call" | custom-call | flops 69000003584 | tf_op jit(solution)/shard_map/adam_expand/pallas_call | solution.py:292
  (420 shorter events, 269.1 us)
Async XLA Ops:
  15.3 46.4 %all-to-all-start = ((bf16[4,144,896]{2,1,0:T(8,128)(2,1)}), bf16[4,144,896]{2,1,0:T(8,128)(2,1)S(1)}, u32[]{:S(2)}, u32[]{:S(2)}) async-start(bf16[4,144,896]{2,1,0:T(8,128)(2,1)} %maximum_select_fusion.1), calls=%async_computation | async-start | bytes 2064384 | tf_op jit(solution)/shard_map/all_to_all | solution.py:140
  21.5 49.0 %all-gather.4.cloned.1.call-start = ((), (), s32[]{:S(2)}) async-start(), calls=%async_computation.9 | async-start | bytes 1474560 | tf_op jit(solution)/shard_map/all_gather | solution.py:682
  61.7 33.0 %all-to-all-start.1 = ((bf16[4,144,1152]{2,1,0:T(8,128)(2,1)}), bf16[4,144,1152]{2,1,0:T(8,128)(2,1)}, u32[]{:S(2)}, u32[]{:S(2)}) async-start(bf16[4,144,1152]{2,1,0:T(8,128)(2,1)} %get-tuple-element.68), calls=%async_computation.1 | async-start | bytes 2654208 | tf_op jit(solution)/shard_map/all_to_all | solution.py:140
  66.0 177.5 %all-gather.6.cloned.1.call-start = ((), (), s32[]{:S(2)}) async-start(), calls=%async_computation.10 | async-start | bytes 6635520 | tf_op jit(solution)/shard_map/all_gather | solution.py:175
  68.0 17.5 %collective-permute-start.2 = (bf16[4,144,640]{2,1,0:T(8,128)(2,1)}, bf16[4,144,640]{2,1,0:T(8,128)(2,1)S(1)}, u32[]{:S(2)}, u32[]{:S(2)}) collective-permute-start(bf16[4,144,640]{2,1,0:T(8,128)(2,1)} %slice.180), channel_id=1, source_target_pairs={{0,2},{1,5},{2,0},{3,7},{4,6},{5,1},{6,4},{7,3},{8,10},{9,13},{10,... | collective-permute-start | bytes 2211848 | tf_op jit(solution)/shard_map/ppermute | solution.py:112
  70.5 18.6 %collective-permute-start = (bf16[256,2304]{1,0:T(8,128)(2,1)}, bf16[256,2304]{1,0:T(8,128)(2,1)S(1)}, u32[]{:S(2)}, u32[]{:S(2)}) collective-permute-start(bf16[256,2304]{1,0:T(8,128)(2,1)} %all-gather.4.cloned.1.call-done), channel_id=1, source_target_pairs={{0,1},{1,0},{2,3},{3,2},{4,5},{5,4},{6,7},{7,6},{8,9},{9,8},{10,11... | collective-permute-start | bytes 3538952 | tf_op jit(solution)/shard_map/ppermute | solution.py:104
  70.5 17.6 %collective-permute-start.3 = (bf16[4,144,640]{2,1,0:T(8,128)(2,1)}, bf16[4,144,640]{2,1,0:T(8,128)(2,1)S(1)}, u32[]{:S(2)}, u32[]{:S(2)}) collective-permute-start(bf16[4,144,640]{2,1,0:T(8,128)(2,1)} %slice.180), channel_id=1, source_target_pairs={{0,4},{1,3},{2,6},{3,1},{4,0},{5,7},{6,2},{7,5},{8,12},{9,11},{10,... | collective-permute-start | bytes 2211848 | tf_op jit(solution)/shard_map/ppermute | solution.py:112
  85.5 16.0 %collective-permute-start.4 = (bf16[4,144,640]{2,1,0:T(8,128)(2,1)S(1)}, bf16[4,144,640]{2,1,0:T(8,128)(2,1)}, u32[]{:S(2)}, u32[]{:S(2)}) collective-permute-start(bf16[4,144,640]{2,1,0:T(8,128)(2,1)S(1)} %collective-permute-done.2), channel_id=1, source_target_pairs={{0,4},{1,3},{2,6},{3,1},{4,0},{5,7},{6,2},{7,5},{8,12},{9,11},{10,... | collective-permute-start | bytes 2211848 | tf_op jit(solution)/shard_map/ppermute | solution.py:112
  97.7 63.3 %all-to-all-start.2 = ((bf16[4,144,2304]{2,1,0:T(8,128)(2,1)}), bf16[4,144,2304]{2,1,0:T(8,128)(2,1)S(1)}, u32[]{:S(2)}, u32[]{:S(2)}) async-start(bf16[4,144,2304]{2,1,0:T(8,128)(2,1)} %pad_maximum_fusion.1), calls=%async_computation.2 | async-start | bytes 5308416 | tf_op jit(solution)/shard_map/all_to_all | solution.py:140
  101.5 169.3 %all-gather.8.cloned.1.call-start = ((), (), s32[]{:S(2)}) async-start(), calls=%async_computation.11 | async-start | bytes 13271040 | tf_op jit(solution)/shard_map/all_gather | solution.py:175
  119.1 43.5 %collective-permute-start.6 = (bf16[512,256]{1,0:T(8,128)(2,1)}, bf16[512,256]{1,0:T(8,128)(2,1)}, u32[]{:S(2)}, u32[]{:S(2)}) collective-permute-start(bf16[512,256]{1,0:T(8,128)(2,1)} %get-tuple-element.164), channel_id=1, source_target_pairs={{0,4},{1,3},{2,6},{3,1},{4,0},{5,7},{6,2},{7,5},{8,12},{9,11},{10,... | collective-permute-start | bytes 786440 | tf_op jit(solution)/shard_map/ppermute | solution.py:112
  125.5 38.9 %collective-permute-start.7 = (bf16[512,256]{1,0:T(8,128)(2,1)}, bf16[512,256]{1,0:T(8,128)(2,1)}, u32[]{:S(2)}, u32[]{:S(2)}) collective-permute-start(bf16[512,256]{1,0:T(8,128)(2,1)} %collective-permute-done.5), channel_id=1, source_target_pairs={{0,4},{1,3},{2,6},{3,1},{4,0},{5,7},{6,2},{7,5},{8,12},{9,11},{10,... | collective-permute-start | bytes 786440 | tf_op jit(solution)/shard_map/ppermute | solution.py:112
  162.6 282.6 %reduce-scatter.4.cloned.1.call-start = ((), (), s32[]{:S(2)}) async-start(), calls=%async_computation.12 | async-start | bytes 6635520 | tf_op jit(solution)/shard_map/reduce_scatter | solution.py:180
  167.5 17.1 %collective-permute-start.8 = (bf16[2048,256]{1,0:T(8,128)(2,1)}, bf16[2048,256]{1,0:T(8,128)(2,1)S(1)}, u32[]{:S(2)}, u32[]{:S(2)}) collective-permute-start(bf16[2048,256]{1,0:T(8,128)(2,1)} %bitcast.252), channel_id=1, source_target_pairs={{0,1},{1,0},{2,3},{3,2},{4,5},{5,4},{6,7},{7,6},{8,9},{9,8},{10,11... | collective-permute-start | bytes 3145736 | tf_op jit(solution)/shard_map/ppermute | solution.py:104
  171.4 13.2 %collective-permute-start.11 = (bf16[4,144,256]{2,1,0:T(8,128)(2,1)S(1)}, bf16[4,144,256]{2,1,0:T(8,128)(2,1)S(1)}, u32[]{:S(2)}, u32[]{:S(2)}) collective-permute-start(bf16[4,144,256]{2,1,0:T(8,128)(2,1)S(1)} %collective-permute-done.9), channel_id=1, source_target_pairs={{0,4},{1,3},{2,6},{3,1},{4,0},{5,7},{6,2},{7,5},{8,12},{9,11},{10,... | collective-permute-start | bytes 884744 | tf_op jit(solution)/shard_map/ppermute | solution.py:112
  195.0 21.9 %collective-permute-start.13 = (bf16[64,2304]{1,0:T(8,128)(2,1)S(1)}, bf16[64,2304]{1,0:T(8,128)(2,1)S(1)}, u32[]{:S(2)}, u32[]{:S(2)}) collective-permute-start(bf16[64,2304]{1,0:T(8,128)(2,1)S(1)} %get-tuple-element.174), channel_id=1, source_target_pairs={{0,8},{8,0},{16,24},{24,16},{1,9},{9,1},{17,25},{25,17},{2,10},{10... | collective-permute-start | bytes 884744 | tf_op jit(solution)/shard_map/ppermute | solution.py:101
  221.0 15.1 %collective-permute-start.16 = (bf16[64,2304]{1,0:T(8,128)(2,1)S(1)}, bf16[64,2304]{1,0:T(8,128)(2,1)S(1)}, u32[]{:S(2)}, u32[]{:S(2)}) collective-permute-start(bf16[64,2304]{1,0:T(8,128)(2,1)S(1)} %get-tuple-element.158), channel_id=1, source_target_pairs={{0,8},{8,0},{16,24},{24,16},{1,9},{9,1},{17,25},{25,17},{2,10},{10... | collective-permute-start | bytes 884744 | tf_op jit(solution)/shard_map/ppermute | solution.py:101
  230.6 12.8 %collective-permute-start.18 = (bf16[64,2304]{1,0:T(8,128)(2,1)S(1)}, bf16[64,2304]{1,0:T(8,128)(2,1)S(1)}, u32[]{:S(2)}, u32[]{:S(2)}) collective-permute-start(bf16[64,2304]{1,0:T(8,128)(2,1)S(1)} %collective-permute-done.17), channel_id=1, source_target_pairs={{0,8},{8,0},{16,24},{24,16},{1,9},{9,1},{17,25},{25,17},{2,10},{10... | collective-permute-start | bytes 884744 | tf_op jit(solution)/shard_map/ppermute | solution.py:101
  290.0 13.8 %collective-permute-start.21 = (bf16[64,2304]{1,0:T(8,128)(2,1)S(1)}, bf16[64,2304]{1,0:T(8,128)(2,1)S(1)}, u32[]{:S(2)}, u32[]{:S(2)}) collective-permute-start(bf16[64,2304]{1,0:T(8,128)(2,1)S(1)} %get-tuple-element.172), channel_id=1, source_target_pairs={{0,8},{8,0},{16,24},{24,16},{1,9},{9,1},{17,25},{25,17},{2,10},{10... | collective-permute-start | bytes 884744 | tf_op jit(solution)/shard_map/ppermute | solution.py:101
  298.4 13.7 %collective-permute-start.23 = (bf16[64,2304]{1,0:T(8,128)(2,1)S(1)}, bf16[64,2304]{1,0:T(8,128)(2,1)S(1)}, u32[]{:S(2)}, u32[]{:S(2)}) collective-permute-start(bf16[64,2304]{1,0:T(8,128)(2,1)S(1)} %fusion.43), channel_id=1, source_target_pairs={{0,24},{8,16},{16,8},{24,0},{1,25},{9,17},{17,9},{25,1},{2,26},{10... | collective-permute-start | bytes 884744 | tf_op jit(solution)/shard_map/ppermute | solution.py:101
  315.7 15.0 %collective-permute-start.25 = (bf16[64,2304]{1,0:T(8,128)(2,1)S(1)}, bf16[64,2304]{1,0:T(8,128)(2,1)S(1)}, u32[]{:S(2)}, u32[]{:S(2)}) collective-permute-start(bf16[64,2304]{1,0:T(8,128)(2,1)S(1)} %get-tuple-element.154), channel_id=1, source_target_pairs={{0,8},{8,0},{16,24},{24,16},{1,9},{9,1},{17,25},{25,17},{2,10},{10... | collective-permute-start | bytes 884744 | tf_op jit(solution)/shard_map/ppermute | solution.py:101
  344.2 178.6 %reduce-scatter.8.cloned.1.call-start = ((), (), s32[]{:S(2)}) async-start(), calls=%async_computation.14 | async-start | bytes 13271040 | tf_op jit(solution)/shard_map/reduce_scatter | solution.py:180
  377.7 21.7 %collective-permute-start.30 = (bf16[64,2304]{1,0:T(8,128)(2,1)S(1)}, bf16[64,2304]{1,0:T(8,128)(2,1)S(1)}, u32[]{:S(2)}, u32[]{:S(2)}) collective-permute-start(bf16[64,2304]{1,0:T(8,128)(2,1)S(1)} %get-tuple-element.168), channel_id=1, source_target_pairs={{0,8},{8,0},{16,24},{24,16},{1,9},{9,1},{17,25},{25,17},{2,10},{10... | collective-permute-start | bytes 884744 | tf_op jit(solution)/shard_map/ppermute | solution.py:101
  403.5 14.0 %collective-permute-start.33 = (bf16[64,2304]{1,0:T(8,128)(2,1)S(1)}, bf16[64,2304]{1,0:T(8,128)(2,1)S(1)}, u32[]{:S(2)}, u32[]{:S(2)}) collective-permute-start(bf16[64,2304]{1,0:T(8,128)(2,1)S(1)} %get-tuple-element.150), channel_id=1, source_target_pairs={{0,8},{8,0},{16,24},{24,16},{1,9},{9,1},{17,25},{25,17},{2,10},{10... | collective-permute-start | bytes 884744 | tf_op jit(solution)/shard_map/ppermute | solution.py:101
  445.2 35.5 %all-to-all-start.3 = ((bf16[4,144,1152]{2,1,0:T(8,128)(2,1)}), bf16[4,144,1152]{2,1,0:T(8,128)(2,1)S(1)}, u32[]{:S(2)}, u32[]{:S(2)}) async-start(bf16[4,144,1152]{2,1,0:T(8,128)(2,1)} %reduce-scatter.4.cloned.1.call-done), calls=%async_computation.4 | async-start | bytes 2654208 | tf_op jit(solution)/shard_map/all_to_all | solution.py:140
  448.8 128.0 %reduce-scatter.6.cloned.1.call-start = ((), (), s32[]{:S(2)}) async-start(), calls=%async_computation.13 | async-start | bytes 5160960 | tf_op jit(solution)/shard_map/reduce_scatter | solution.py:180
  448.8 17.7 %collective-permute-start.38 = (bf16[512,256]{1,0:T(8,128)(2,1)S(1)}, bf16[512,256]{1,0:T(8,128)(2,1)S(1)}, u32[]{:S(2)}, u32[]{:S(2)}) collective-permute-start(bf16[512,256]{1,0:T(8,128)(2,1)S(1)} %get-tuple-element.182), channel_id=1, source_target_pairs={{0,4},{1,3},{2,6},{3,1},{4,0},{5,7},{6,2},{7,5},{8,12},{9,11},{10,... | collective-permute-start | bytes 786440 | tf_op jit(solution)/shard_map/ppermute | solution.py:112
  457.4 13.0 %collective-permute-start.40 = (bf16[512,256]{1,0:T(8,128)(2,1)S(1)}, bf16[512,256]{1,0:T(8,128)(2,1)S(1)}, u32[]{:S(2)}, u32[]{:S(2)}) collective-permute-start(bf16[512,256]{1,0:T(8,128)(2,1)S(1)} %fusion.53), channel_id=1, source_target_pairs={{0,2},{1,5},{2,0},{3,7},{4,6},{5,1},{6,4},{7,3},{8,10},{9,13},{10,... | collective-permute-start | bytes 786440 | tf_op jit(solution)/shard_map/ppermute | solution.py:112
  501.4 20.8 %collective-permute-start.42 = (bf16[64,2304]{1,0:T(8,128)(2,1)S(1)}, bf16[64,2304]{1,0:T(8,128)(2,1)S(1)}, u32[]{:S(2)}, u32[]{:S(2)}) collective-permute-start(bf16[64,2304]{1,0:T(8,128)(2,1)S(1)} %get-tuple-element.166), channel_id=1, source_target_pairs={{0,8},{8,0},{16,24},{24,16},{1,9},{9,1},{17,25},{25,17},{2,10},{10... | collective-permute-start | bytes 884744 | tf_op jit(solution)/shard_map/ppermute | solution.py:101
  522.7 16.3 %collective-permute-start.45 = (f32[64,2304]{1,0:T(8,128)S(1)}, f32[64,2304]{1,0:T(8,128)}, u32[]{:S(2)}, u32[]{:S(2)}) collective-permute-start(f32[64,2304]{1,0:T(8,128)S(1)} %last_grad.1), channel_id=1, source_target_pairs={{0,1},{1,0},{2,3},{3,2},{4,5},{5,4},{6,7},{7,6},{8,9},{9,8},{10,11... | collective-permute-start | bytes 1769480 | tf_op jit(solution)/shard_map/ppermute | solution.py:104
  522.8 65.7 %all-to-all-start.4 = ((bf16[4,144,2304]{2,1,0:T(8,128)(2,1)}), bf16[4,144,2304]{2,1,0:T(8,128)(2,1)}, u32[]{:S(2)}, u32[]{:S(2)}) async-start(bf16[4,144,2304]{2,1,0:T(8,128)(2,1)} %reduce-scatter.8.cloned.1.call-done), calls=%async_computation.7 | async-start | bytes 5308416 | tf_op jit(solution)/shard_map/all_to_all | solution.py:140
  588.5 29.2 %all-to-all-start.5 = ((bf16[4,144,896]{2,1,0:T(8,128)(2,1)}), bf16[4,144,896]{2,1,0:T(8,128)(2,1)S(1)}, u32[]{:S(2)}, u32[]{:S(2)}) async-start(bf16[4,144,896]{2,1,0:T(8,128)(2,1)} %reduce-scatter.6.cloned.1.call-done), calls=%async_computation.8 | async-start | bytes 2064384 | tf_op jit(solution)/shard_map/all_to_all | solution.py:140
  (113 other events, 1021.0 us)
Sparse Core Ops, SparseCore 0:
  24.5 45.9 all-gather.3
Sparse Core Ops, SparseCore 1:
  94.8 64.4 all-gather.5
  162.7 108.1 all-gather.7
  344.3 60.6 reduce-scatter.3
  408.1 112.9 reduce-scatter.7
  524.7 52.0 reduce-scatter.5

commit v3 on v1

--- a/solution.py
+++ b/solution.py
@@ -406,7 +406,7 @@
     return [a.T for a in results]
 
 
-LINE_WEIGHT = 60
+LINE_WEIGHT = 90
 OWN_WEIGHT = 3
 
 
@@ -812,7 +812,7 @@
     grad_query_pre = rotate(grad_query, cosine, -sine_table)
     grad_pair_pre = jnp.where(core == 0, rotate(pair_grad, cosine, -sine_table), pair_grad)
     grad_proj_b = jnp.concatenate([grad_query_pre, grad_pair_pre], axis=1).astype(BF16)
-    shrink_back = grid.line_swap(after(shrink_sums, grad_attend_line))
+    shrink_back = grid.line_swap(shrink_sums)
     own_part, other_part = halves_last((after(grad_proj_b, shrink_back), attend_full))
     gain_one = jnp.sum(own_part * normed_plain[:half], axis=0) + jnp.sum(
         other_part.astype(F32) * normed_plain[half:], axis=0

time: 643 us -> 643 us (level)
  no operation moved by 1% of the time
where the time goes in v3:
time: 643 us; the launch traced here: 635 us
  waiting for transfers between devices  326 us (51%)
  starting transfers between devices  84.6 us (13%)
  Pallas kernels  63.6 us (10%)
  local copies, waits for them, and re-layouts  62.5 us (10%)
  matrix products  43.2 us (7%)
  other arithmetic  37.7 us (6%)
  between operations  17.5 us (3%)
    ppermute x21, waiting for transfers between devices, along(): return lax.ppermute(value, 'line', pairs)  118 us
    all_to_all x6, waiting for transfers between devices, line_swap(): lax.all_to_all(blocks, 'line', split_axis=0, concat_axis=0, tiled=True)  88.5 us
    ppermute x12, waiting for transfers between devices, within(): return lax.ppermute(value, ('place', 'head'), pairs)  40.3 us
    ppermute x21, starting transfers between devices, along(): return lax.ppermute(value, 'line', pairs)  37.6 us
    unnamed x169, local copies, waits for them, and re-layouts  37.3 us
    reduce_scatter x3, waiting for transfers between devices, bulk_sum(): return lax.psum_scatter(shaped, 'place', scatter_dimension=1, tiled=True)  35.3 us
    pallas_call x3, Pallas kernels, adam_call(): pl.pallas_call(kernel, out_shape=[jax.ShapeDtypeStruct(states[0].shape, F...  28.6 us
    all_to_all x6, starting transfers between devices, line_swap(): lax.all_to_all(blocks, 'line', split_axis=0, concat_axis=0, tiled=True)  26.4 us
  transfers between devices with their start and end apart: 61, of which 43 were waited for; matrix products, arithmetic and copies ran while one was open for 15% of the time, Pallas kernels for 8%

profile of v3, /device:TPU:0, one launch (start us, length us, event | category | flops | bytes accessed | tf_op | source)
XLA Modules:
  0.0 634.7 jit_solution(5912759041753370149)
XLA Ops:
  14.1 6.2 all-to-all-start
  24.1 6.2 pack_expand.1
  31.4 29.1 %all-to-all-done = bf16[4,144,896]{2,1,0:T(8,128)(2,1)S(1)} async-done(((bf16[4,144,896]{2,1,0:T(8,128)(2,1)}), bf16[4,144,896]{2,1,0:T(8,128)(2,1)S(1)}, u32[]{:S(2)}, u32[]{:S(2)}) %all-to-all-start) | async-done | bytes 1032224 | tf_op jit(solution)/shard_map/all_to_all | solution.py:140
  77.8 6.6 %collective-permute-done.2 = bf16[4,144,640]{2,1,0:T(8,128)(2,1)S(1)} collective-permute-done((bf16[4,144,640]{2,1,0:T(8,128)(2,1)}, bf16[4,144,640]{2,1,0:T(8,128)(2,1)S(1)}, u32[]{:S(2)}, u32[]{:S(2)}) %collective-permute-start.2) | collective-permute-done | bytes 737312 | tf_op jit(solution)/shard_map/ppermute | solution.py:112
  127.9 32.0 %all-to-all-done.2 = bf16[4,144,2304]{2,1,0:T(8,128)(2,1)S(1)} async-done(((bf16[4,144,2304]{2,1,0:T(8,128)(2,1)}), bf16[4,144,2304]{2,1,0:T(8,128)(2,1)S(1)}, u32[]{:S(2)}, u32[]{:S(2)}) %all-to-all-start.2) | async-done | bytes 2654240 | tf_op jit(solution)/shard_map/all_to_all | solution.py:140
  173.9 9.4 %collective-permute-done.11 = bf16[4,144,256]{2,1,0:T(8,128)(2,1)S(1)} collective-permute-done((bf16[4,144,256]{2,1,0:T(8,128)(2,1)S(1)}, bf16[4,144,256]{2,1,0:T(8,128)(2,1)S(1)}, u32[]{:S(2)}, u32[]{:S(2)}) %collective-permute-start.11) | collective-permute-done | bytes 294944 | tf_op jit(solution)/shard_map/ppermute | solution.py:112
  195.9 7.8 %collective-permute-done.14 = bf16[64,2304]{1,0:T(8,128)(2,1)S(1)} collective-permute-done((bf16[64,2304]{1,0:T(8,128)(2,1)S(1)}, bf16[64,2304]{1,0:T(8,128)(2,1)S(1)}, u32[]{:S(2)}, u32[]{:S(2)}) %collective-permute-start.14) | collective-permute-done | bytes 294944 | tf_op jit(solution)/shard_map/ppermute | solution.py:101
  204.9 10.9 %collective-permute-done.13 = bf16[64,2304]{1,0:T(8,128)(2,1)S(1)} collective-permute-done((bf16[64,2304]{1,0:T(8,128)(2,1)S(1)}, bf16[64,2304]{1,0:T(8,128)(2,1)S(1)}, u32[]{:S(2)}, u32[]{:S(2)}) %collective-permute-start.13) | collective-permute-done | bytes 294944 | tf_op jit(solution)/shard_map/ppermute | solution.py:101
  221.9 7.5 %collective-permute-done.17 = bf16[64,2304]{1,0:T(8,128)(2,1)S(1)} collective-permute-done((bf16[64,2304]{1,0:T(8,128)(2,1)S(1)}, bf16[64,2304]{1,0:T(8,128)(2,1)S(1)}, u32[]{:S(2)}, u32[]{:S(2)}) %collective-permute-start.17) | collective-permute-done | bytes 294944 | tf_op jit(solution)/shard_map/ppermute | solution.py:101
  234.9 7.3 %collective-permute-done.18 = bf16[64,2304]{1,0:T(8,128)(2,1)S(1)} collective-permute-done((bf16[64,2304]{1,0:T(8,128)(2,1)S(1)}, bf16[64,2304]{1,0:T(8,128)(2,1)S(1)}, u32[]{:S(2)}, u32[]{:S(2)}) %collective-permute-start.18) | collective-permute-done | bytes 294944 | tf_op jit(solution)/shard_map/ppermute | solution.py:101
  246.7 23.0 %all-gather.8.cloned.1.call-done = bf16[4,576,2304]{2,1,0:T(8,128)(2,1)} async-done(((bf16[4,144,2304]{2,1,0:T(8,128)(2,1)}), bf16[4,576,2304]{2,1,0:T(8,128)(2,1)}) %all-gather.8.cloned.1.call-update) | async-done | bytes 10616848 | tf_op jit(solution)/shard_map/all_gather | solution.py:175
  273.8 8.5 %gate_and_up.1 = (f32[512,1152]{1,0:T(8,128)S(1)}, f32[512,1152]{1,0:T(8,128)S(1)}, bf16[512,1152]{1,0:T(8,128)(2,1)S(1)}) custom-call(bf16[512,2304]{1,0:T(8,128)(2,1)S(1)} %copy-done.21, bf16[2304,1152]{1,0:T(8,128)(2,1)S(1)} %bitcast.260, bf16[2304,2304]{1,0:T(8,128)(2,1)} %bitcast.245), custom_call_target="tpu_custom_call" | custom-call | flops 5435817984 | bytes 10616832 | tf_op jit(solution)/shard_map/gate_and_up/pallas_call | solution.py:621
  289.4 7.8 %collective-permute-done.22 = bf16[64,2304]{1,0:T(8,128)(2,1)S(1)} collective-permute-done((bf16[64,2304]{1,0:T(8,128)(2,1)S(1)}, bf16[64,2304]{1,0:T(8,128)(2,1)S(1)}, u32[]{:S(2)}, u32[]{:S(2)}) %collective-permute-start.22) | collective-permute-done | bytes 294944 | tf_op jit(solution)/shard_map/ppermute | solution.py:101
  302.7 8.3 %collective-permute-done.23 = bf16[64,2304]{1,0:T(8,128)(2,1)S(1)} collective-permute-done((bf16[64,2304]{1,0:T(8,128)(2,1)S(1)}, bf16[64,2304]{1,0:T(8,128)(2,1)S(1)}, u32[]{:S(2)}, u32[]{:S(2)}) %collective-permute-start.23) | collective-permute-done | bytes 294944 | tf_op jit(solution)/shard_map/ppermute | solution.py:101
  318.1 6.9 %collective-permute-done.26 = bf16[64,2304]{1,0:T(8,128)(2,1)S(1)} collective-permute-done((bf16[64,2304]{1,0:T(8,128)(2,1)S(1)}, bf16[64,2304]{1,0:T(8,128)(2,1)S(1)}, u32[]{:S(2)}, u32[]{:S(2)}) %collective-permute-start.26) | collective-permute-done | bytes 294944 | tf_op jit(solution)/shard_map/ppermute | solution.py:101
  350.4 6.4 %gate_and_up_back.1 = bf16[512,2304]{1,0:T(8,128)(2,1)S(1)} custom-call(bf16[512,2304]{1,0:T(8,128)(2,1)S(1)} %pad_maximum_fusion.3.feed_ref, f32[512,1152]{1,0:T(8,128)S(1)} %get-tuple-element.82.gate_ref, f32[512,1152]{1,0:T(8,128)S(1)} %copy-done.8, bf16[2304,2304]{1,0:T(8,128)(2,1)S(1)} %bitcast.248), custom_call_target="tpu_custom_call" | custom-call | flops 2717908992 | bytes 5308416 | tf_op jit(solution)/shard_map/gate_and_up_back/pallas_call | solution.py:655
  356.9 8.3 %convolution_convert_fusion = bf16[2304,2304]{1,0:T(8,128)(2,1)} fusion(bf16[512,2304]{1,0:T(8,128)(2,1)S(1)} %copy-done.22, bf16[512,2304]{1,0:T(8,128)(2,1)S(1)} %gate_and_up_back.1), kind=kOutput, calls=%fused_computation | convolution fusion | flops 5441126400 | bytes 15335424 | tf_op jit(solution)/shard_map/dot_general | solution.py:591
  378.6 7.8 %collective-permute-done.31 = bf16[64,2304]{1,0:T(8,128)(2,1)S(1)} collective-permute-done((bf16[64,2304]{1,0:T(8,128)(2,1)S(1)}, bf16[64,2304]{1,0:T(8,128)(2,1)S(1)}, u32[]{:S(2)}, u32[]{:S(2)}) %collective-permute-start.31) | collective-permute-done | bytes 294944 | tf_op jit(solution)/shard_map/ppermute | solution.py:101
  387.4 10.8 %collective-permute-done.30 = bf16[64,2304]{1,0:T(8,128)(2,1)S(1)} collective-permute-done((bf16[64,2304]{1,0:T(8,128)(2,1)S(1)}, bf16[64,2304]{1,0:T(8,128)(2,1)S(1)}, u32[]{:S(2)}, u32[]{:S(2)}) %collective-permute-start.30) | collective-permute-done | bytes 294944 | tf_op jit(solution)/shard_map/ppermute | solution.py:101
  403.1 8.8 %collective-permute-done.34 = bf16[64,2304]{1,0:T(8,128)(2,1)S(1)} collective-permute-done((bf16[64,2304]{1,0:T(8,128)(2,1)S(1)}, bf16[64,2304]{1,0:T(8,128)(2,1)S(1)}, u32[]{:S(2)}, u32[]{:S(2)}) %collective-permute-start.34) | collective-permute-done | bytes 294944 | tf_op jit(solution)/shard_map/ppermute | solution.py:101
  416.4 6.8 %collective-permute-done.35 = bf16[64,2304]{1,0:T(8,128)(2,1)S(1)} collective-permute-done((bf16[64,2304]{1,0:T(8,128)(2,1)S(1)}, bf16[64,2304]{1,0:T(8,128)(2,1)S(1)}, u32[]{:S(2)}, u32[]{:S(2)}) %collective-permute-start.35) | collective-permute-done | bytes 294944 | tf_op jit(solution)/shard_map/ppermute | solution.py:101
  427.8 9.6 %attend_backward.1 = (f32[512,256]{1,0:T(8,128)}, f32[2048,256]{1,0:T(8,128)}, bf16[2048,256]{1,0:T(8,128)(2,1)}) custom-call(s32[1]{0:T(128)} %bitcast.core_ref, bf16[512,256]{1,0:T(8,128)(2,1)} %copy-done.25, bf16[2048,256]{1,0:T(8,128)(2,1)} %copy-done.19, bf16[2048,256]{1,0:T(8,128)(2,1)} %copy-done.18, s32[512,1]{1,0:T(8,128)} %broadcast_select_fusion.2.spot_ref, ...), custom_call_target="tpu_custom_call" | custom-call | flops 115000000512 | tf_op jit(solution)/shard_map/attend_backward/pallas_call | solution.py:555
  448.8 6.5 %collective-permute-done.39 = bf16[512,256]{1,0:T(8,128)(2,1)} collective-permute-done((bf16[512,256]{1,0:T(8,128)(2,1)}, bf16[512,256]{1,0:T(8,128)(2,1)}, u32[]{:S(2)}, u32[]{:S(2)}) %collective-permute-start.39) | collective-permute-done | bytes 262176 | tf_op jit(solution)/shard_map/ppermute | solution.py:112
  458.7 6.7 %collective-permute-done.38 = bf16[512,256]{1,0:T(8,128)(2,1)S(1)} collective-permute-done((bf16[512,256]{1,0:T(8,128)(2,1)S(1)}, bf16[512,256]{1,0:T(8,128)(2,1)S(1)}, u32[]{:S(2)}, u32[]{:S(2)}) %collective-permute-start.38) | collective-permute-done | bytes 262176 | tf_op jit(solution)/shard_map/ppermute | solution.py:112
  472.7 6.9 %all-to-all-done.3.grad_ref = bf16[4,144,1152]{2,1,0:T(8,128)(2,1)S(1)} async-done(((bf16[4,144,1152]{2,1,0:T(8,128)(2,1)}), bf16[4,144,1152]{2,1,0:T(8,128)(2,1)S(1)}, u32[]{:S(2)}, u32[]{:S(2)}) %all-to-all-start.3) | async-done | bytes 1327136 | tf_op jit(solution)/shard_map/all_to_all | solution.py:140
  492.7 6.4 %copy.159 = bf16[2304,896]{1,0:T(8,128)(2,1)} copy(bf16[2304,896]{0,1:T(8,128)(2,1)} %pad_maximum_fusion) | data formatting | bytes 8257536 | tf_op jit(solution)/shard_map/concatenate | solution.py:827
  501.4 7.8 %collective-permute-done.43 = bf16[64,2304]{1,0:T(8,128)(2,1)S(1)} collective-permute-done((bf16[64,2304]{1,0:T(8,128)(2,1)S(1)}, bf16[64,2304]{1,0:T(8,128)(2,1)S(1)}, u32[]{:S(2)}, u32[]{:S(2)}) %collective-permute-start.43) | collective-permute-done | bytes 294944 | tf_op jit(solution)/shard_map/ppermute | solution.py:101
  511.8 9.2 %collective-permute-done.42 = bf16[64,2304]{1,0:T(8,128)(2,1)S(1)} collective-permute-done((bf16[64,2304]{1,0:T(8,128)(2,1)S(1)}, bf16[64,2304]{1,0:T(8,128)(2,1)S(1)}, u32[]{:S(2)}, u32[]{:S(2)}) %collective-permute-start.42) | collective-permute-done | bytes 294944 | tf_op jit(solution)/shard_map/ppermute | solution.py:101
  531.7 6.1 adam_shrink.1
  540.3 35.3 %reduce-scatter.6.cloned.1.call-done = bf16[4,144,896]{2,1,0:T(8,128)(2,1)} async-done(((bf16[4,576,896]{2,1,0:T(8,128)(2,1)}), bf16[4,144,896]{2,1,0:T(8,128)(2,1)}) %reduce-scatter.6.cloned.1.call-update) | async-done | bytes 1032208 | tf_op jit(solution)/shard_map/reduce_scatter | solution.py:180
  575.6 11.8 %all-to-all-done.4.grad_ref = bf16[4,144,2304]{2,1,0:T(8,128)(2,1)} async-done(((bf16[4,144,2304]{2,1,0:T(8,128)(2,1)}), bf16[4,144,2304]{2,1,0:T(8,128)(2,1)}, u32[]{:S(2)}, u32[]{:S(2)}) %all-to-all-start.4) | async-done | bytes 2654240 | tf_op jit(solution)/shard_map/all_to_all | solution.py:140
  596.2 17.1 %adam_expand.1 = (f32[144,2,4608]{2,1,0:T(2,128)}, f32[144,2,4608]{2,1,0:T(2,128)}, f32[144,2,4608]{2,1,0:T(2,128)}, f32[144,2,4608]{2,1,0:T(2,128)}) custom-call(bf16[4,144,2304]{2,1,0:T(8,128)(2,1)} %all-to-all-done.4.grad_ref, f32[144,2,4608]{2,1,0:T(2,128)S(1)} %copy-done.4, f32[144,2,4608]{2,1,0:T(2,128)S(1)} %copy-done.28, f32[144,2,4608]{2,1,0:T(2,128)} %refs_2_.1), custom_call_target="tpu_custom_call" | custom-call | flops 69000003584 | tf_op jit(solution)/shard_map/adam_expand/pallas_call | solution.py:312
  (420 shorter events, 267.2 us)
Async XLA Ops:
  14.1 46.4 %all-to-all-start = ((bf16[4,144,896]{2,1,0:T(8,128)(2,1)}), bf16[4,144,896]{2,1,0:T(8,128)(2,1)S(1)}, u32[]{:S(2)}, u32[]{:S(2)}) async-start(bf16[4,144,896]{2,1,0:T(8,128)(2,1)} %maximum_select_fusion.1), calls=%async_computation | async-start | bytes 2064384 | tf_op jit(solution)/shard_map/all_to_all | solution.py:140
  20.3 49.0 %all-gather.4.cloned.1.call-start = ((), (), s32[]{:S(2)}) async-start(), calls=%async_computation.9 | async-start | bytes 1474560 | tf_op jit(solution)/shard_map/all_gather | solution.py:706
  60.5 33.0 %all-to-all-start.1 = ((bf16[4,144,1152]{2,1,0:T(8,128)(2,1)}), bf16[4,144,1152]{2,1,0:T(8,128)(2,1)}, u32[]{:S(2)}, u32[]{:S(2)}) async-start(bf16[4,144,1152]{2,1,0:T(8,128)(2,1)} %get-tuple-element.67), calls=%async_computation.1 | async-start | bytes 2654208 | tf_op jit(solution)/shard_map/all_to_all | solution.py:140
  64.8 177.5 %all-gather.6.cloned.1.call-start = ((), (), s32[]{:S(2)}) async-start(), calls=%async_computation.10 | async-start | bytes 6635520 | tf_op jit(solution)/shard_map/all_gather | solution.py:175
  66.9 17.5 %collective-permute-start.2 = (bf16[4,144,640]{2,1,0:T(8,128)(2,1)}, bf16[4,144,640]{2,1,0:T(8,128)(2,1)S(1)}, u32[]{:S(2)}, u32[]{:S(2)}) collective-permute-start(bf16[4,144,640]{2,1,0:T(8,128)(2,1)} %slice.180), channel_id=1, source_target_pairs={{0,2},{1,5},{2,0},{3,7},{4,6},{5,1},{6,4},{7,3},{8,10},{9,13},{10,... | collective-permute-start | bytes 2211848 | tf_op jit(solution)/shard_map/ppermute | solution.py:112
  69.3 18.6 %collective-permute-start = (bf16[256,2304]{1,0:T(8,128)(2,1)}, bf16[256,2304]{1,0:T(8,128)(2,1)S(1)}, u32[]{:S(2)}, u32[]{:S(2)}) collective-permute-start(bf16[256,2304]{1,0:T(8,128)(2,1)} %all-gather.4.cloned.1.call-done), channel_id=1, source_target_pairs={{0,1},{1,0},{2,3},{3,2},{4,5},{5,4},{6,7},{7,6},{8,9},{9,8},{10,11... | collective-permute-start | bytes 3538952 | tf_op jit(solution)/shard_map/ppermute | solution.py:104
  69.4 17.6 %collective-permute-start.3 = (bf16[4,144,640]{2,1,0:T(8,128)(2,1)}, bf16[4,144,640]{2,1,0:T(8,128)(2,1)S(1)}, u32[]{:S(2)}, u32[]{:S(2)}) collective-permute-start(bf16[4,144,640]{2,1,0:T(8,128)(2,1)} %slice.180), channel_id=1, source_target_pairs={{0,4},{1,3},{2,6},{3,1},{4,0},{5,7},{6,2},{7,5},{8,12},{9,11},{10,... | collective-permute-start | bytes 2211848 | tf_op jit(solution)/shard_map/ppermute | solution.py:112
  84.4 16.0 %collective-permute-start.4 = (bf16[4,144,640]{2,1,0:T(8,128)(2,1)S(1)}, bf16[4,144,640]{2,1,0:T(8,128)(2,1)}, u32[]{:S(2)}, u32[]{:S(2)}) collective-permute-start(bf16[4,144,640]{2,1,0:T(8,128)(2,1)S(1)} %collective-permute-done.2), channel_id=1, source_target_pairs={{0,4},{1,3},{2,6},{3,1},{4,0},{5,7},{6,2},{7,5},{8,12},{9,11},{10,... | collective-permute-start | bytes 2211848 | tf_op jit(solution)/shard_map/ppermute | solution.py:112
  96.6 63.3 %all-to-all-start.2 = ((bf16[4,144,2304]{2,1,0:T(8,128)(2,1)}), bf16[4,144,2304]{2,1,0:T(8,128)(2,1)S(1)}, u32[]{:S(2)}, u32[]{:S(2)}) async-start(bf16[4,144,2304]{2,1,0:T(8,128)(2,1)} %pad_maximum_fusion.1), calls=%async_computation.2 | async-start | bytes 5308416 | tf_op jit(solution)/shard_map/all_to_all | solution.py:140
  100.3 169.3 %all-gather.8.cloned.1.call-start = ((), (), s32[]{:S(2)}) async-start(), calls=%async_computation.11 | async-start | bytes 13271040 | tf_op jit(solution)/shard_map/all_gather | solution.py:175
  118.0 43.5 %collective-permute-start.6 = (bf16[512,256]{1,0:T(8,128)(2,1)}, bf16[512,256]{1,0:T(8,128)(2,1)}, u32[]{:S(2)}, u32[]{:S(2)}) collective-permute-start(bf16[512,256]{1,0:T(8,128)(2,1)} %get-tuple-element.162), channel_id=1, source_target_pairs={{0,4},{1,3},{2,6},{3,1},{4,0},{5,7},{6,2},{7,5},{8,12},{9,11},{10,... | collective-permute-start | bytes 786440 | tf_op jit(solution)/shard_map/ppermute | solution.py:112
  124.3 38.9 %collective-permute-start.7 = (bf16[512,256]{1,0:T(8,128)(2,1)}, bf16[512,256]{1,0:T(8,128)(2,1)}, u32[]{:S(2)}, u32[]{:S(2)}) collective-permute-start(bf16[512,256]{1,0:T(8,128)(2,1)} %collective-permute-done.5), channel_id=1, source_target_pairs={{0,4},{1,3},{2,6},{3,1},{4,0},{5,7},{6,2},{7,5},{8,12},{9,11},{10,... | collective-permute-start | bytes 786440 | tf_op jit(solution)/shard_map/ppermute | solution.py:112
  161.4 282.6 %reduce-scatter.4.cloned.1.call-start = ((), (), s32[]{:S(2)}) async-start(), calls=%async_computation.12 | async-start | bytes 6635520 | tf_op jit(solution)/shard_map/reduce_scatter | solution.py:180
  166.3 17.1 %collective-permute-start.8 = (bf16[2048,256]{1,0:T(8,128)(2,1)}, bf16[2048,256]{1,0:T(8,128)(2,1)S(1)}, u32[]{:S(2)}, u32[]{:S(2)}) collective-permute-start(bf16[2048,256]{1,0:T(8,128)(2,1)} %bitcast.291), channel_id=1, source_target_pairs={{0,1},{1,0},{2,3},{3,2},{4,5},{5,4},{6,7},{7,6},{8,9},{9,8},{10,11... | collective-permute-start | bytes 3145736 | tf_op jit(solution)/shard_map/ppermute | solution.py:104
  170.2 13.2 %collective-permute-start.11 = (bf16[4,144,256]{2,1,0:T(8,128)(2,1)S(1)}, bf16[4,144,256]{2,1,0:T(8,128)(2,1)S(1)}, u32[]{:S(2)}, u32[]{:S(2)}) collective-permute-start(bf16[4,144,256]{2,1,0:T(8,128)(2,1)S(1)} %collective-permute-done.9), channel_id=1, source_target_pairs={{0,4},{1,3},{2,6},{3,1},{4,0},{5,7},{6,2},{7,5},{8,12},{9,11},{10,... | collective-permute-start | bytes 884744 | tf_op jit(solution)/shard_map/ppermute | solution.py:112
  193.8 21.9 %collective-permute-start.13 = (bf16[64,2304]{1,0:T(8,128)(2,1)S(1)}, bf16[64,2304]{1,0:T(8,128)(2,1)S(1)}, u32[]{:S(2)}, u32[]{:S(2)}) collective-permute-start(bf16[64,2304]{1,0:T(8,128)(2,1)S(1)} %get-tuple-element.172), channel_id=1, source_target_pairs={{0,8},{8,0},{16,24},{24,16},{1,9},{9,1},{17,25},{25,17},{2,10},{10... | collective-permute-start | bytes 884744 | tf_op jit(solution)/shard_map/ppermute | solution.py:101
  219.8 15.1 %collective-permute-start.16 = (bf16[64,2304]{1,0:T(8,128)(2,1)S(1)}, bf16[64,2304]{1,0:T(8,128)(2,1)S(1)}, u32[]{:S(2)}, u32[]{:S(2)}) collective-permute-start(bf16[64,2304]{1,0:T(8,128)(2,1)S(1)} %get-tuple-element.156), channel_id=1, source_target_pairs={{0,8},{8,0},{16,24},{24,16},{1,9},{9,1},{17,25},{25,17},{2,10},{10... | collective-permute-start | bytes 884744 | tf_op jit(solution)/shard_map/ppermute | solution.py:101
  229.4 12.8 %collective-permute-start.18 = (bf16[64,2304]{1,0:T(8,128)(2,1)S(1)}, bf16[64,2304]{1,0:T(8,128)(2,1)S(1)}, u32[]{:S(2)}, u32[]{:S(2)}) collective-permute-start(bf16[64,2304]{1,0:T(8,128)(2,1)S(1)} %collective-permute-done.17), channel_id=1, source_target_pairs={{0,8},{8,0},{16,24},{24,16},{1,9},{9,1},{17,25},{25,17},{2,10},{10... | collective-permute-start | bytes 884744 | tf_op jit(solution)/shard_map/ppermute | solution.py:101
  288.8 13.9 %collective-permute-start.21 = (bf16[64,2304]{1,0:T(8,128)(2,1)S(1)}, bf16[64,2304]{1,0:T(8,128)(2,1)S(1)}, u32[]{:S(2)}, u32[]{:S(2)}) collective-permute-start(bf16[64,2304]{1,0:T(8,128)(2,1)S(1)} %get-tuple-element.170), channel_id=1, source_target_pairs={{0,8},{8,0},{16,24},{24,16},{1,9},{9,1},{17,25},{25,17},{2,10},{10... | collective-permute-start | bytes 884744 | tf_op jit(solution)/shard_map/ppermute | solution.py:101
  297.3 13.7 %collective-permute-start.23 = (bf16[64,2304]{1,0:T(8,128)(2,1)S(1)}, bf16[64,2304]{1,0:T(8,128)(2,1)S(1)}, u32[]{:S(2)}, u32[]{:S(2)}) collective-permute-start(bf16[64,2304]{1,0:T(8,128)(2,1)S(1)} %fusion.44), channel_id=1, source_target_pairs={{0,24},{8,16},{16,8},{24,0},{1,25},{9,17},{17,9},{25,1},{2,26},{10... | collective-permute-start | bytes 884744 | tf_op jit(solution)/shard_map/ppermute | solution.py:101
  314.6 15.0 %collective-permute-start.25 = (bf16[64,2304]{1,0:T(8,128)(2,1)S(1)}, bf16[64,2304]{1,0:T(8,128)(2,1)S(1)}, u32[]{:S(2)}, u32[]{:S(2)}) collective-permute-start(bf16[64,2304]{1,0:T(8,128)(2,1)S(1)} %get-tuple-element.152), channel_id=1, source_target_pairs={{0,8},{8,0},{16,24},{24,16},{1,9},{9,1},{17,25},{25,17},{2,10},{10... | collective-permute-start | bytes 884744 | tf_op jit(solution)/shard_map/ppermute | solution.py:101
  343.1 178.6 %reduce-scatter.8.cloned.1.call-start = ((), (), s32[]{:S(2)}) async-start(), calls=%async_computation.14 | async-start | bytes 13271040 | tf_op jit(solution)/shard_map/reduce_scatter | solution.py:180
  376.6 21.7 %collective-permute-start.30 = (bf16[64,2304]{1,0:T(8,128)(2,1)S(1)}, bf16[64,2304]{1,0:T(8,128)(2,1)S(1)}, u32[]{:S(2)}, u32[]{:S(2)}) collective-permute-start(bf16[64,2304]{1,0:T(8,128)(2,1)S(1)} %get-tuple-element.166), channel_id=1, source_target_pairs={{0,8},{8,0},{16,24},{24,16},{1,9},{9,1},{17,25},{25,17},{2,10},{10... | collective-permute-start | bytes 884744 | tf_op jit(solution)/shard_map/ppermute | solution.py:101
  402.4 14.0 %collective-permute-start.33 = (bf16[64,2304]{1,0:T(8,128)(2,1)S(1)}, bf16[64,2304]{1,0:T(8,128)(2,1)S(1)}, u32[]{:S(2)}, u32[]{:S(2)}) collective-permute-start(bf16[64,2304]{1,0:T(8,128)(2,1)S(1)} %get-tuple-element.148), channel_id=1, source_target_pairs={{0,8},{8,0},{16,24},{24,16},{1,9},{9,1},{17,25},{25,17},{2,10},{10... | collective-permute-start | bytes 884744 | tf_op jit(solution)/shard_map/ppermute | solution.py:101
  444.1 35.5 %all-to-all-start.3 = ((bf16[4,144,1152]{2,1,0:T(8,128)(2,1)}), bf16[4,144,1152]{2,1,0:T(8,128)(2,1)S(1)}, u32[]{:S(2)}, u32[]{:S(2)}) async-start(bf16[4,144,1152]{2,1,0:T(8,128)(2,1)} %reduce-scatter.4.cloned.1.call-done), calls=%async_computation.4 | async-start | bytes 2654208 | tf_op jit(solution)/shard_map/all_to_all | solution.py:140
  447.6 127.9 %reduce-scatter.6.cloned.1.call-start = ((), (), s32[]{:S(2)}) async-start(), calls=%async_computation.13 | async-start | bytes 5160960 | tf_op jit(solution)/shard_map/reduce_scatter | solution.py:180
  447.7 17.7 %collective-permute-start.38 = (bf16[512,256]{1,0:T(8,128)(2,1)S(1)}, bf16[512,256]{1,0:T(8,128)(2,1)S(1)}, u32[]{:S(2)}, u32[]{:S(2)}) collective-permute-start(bf16[512,256]{1,0:T(8,128)(2,1)S(1)} %get-tuple-element.180), channel_id=1, source_target_pairs={{0,4},{1,3},{2,6},{3,1},{4,0},{5,7},{6,2},{7,5},{8,12},{9,11},{10,... | collective-permute-start | bytes 786440 | tf_op jit(solution)/shard_map/ppermute | solution.py:112
  456.4 13.0 %collective-permute-start.40 = (bf16[512,256]{1,0:T(8,128)(2,1)S(1)}, bf16[512,256]{1,0:T(8,128)(2,1)S(1)}, u32[]{:S(2)}, u32[]{:S(2)}) collective-permute-start(bf16[512,256]{1,0:T(8,128)(2,1)S(1)} %fusion.54), channel_id=1, source_target_pairs={{0,2},{1,5},{2,0},{3,7},{4,6},{5,1},{6,4},{7,3},{8,10},{9,13},{10,... | collective-permute-start | bytes 786440 | tf_op jit(solution)/shard_map/ppermute | solution.py:112
  500.2 20.8 %collective-permute-start.42 = (bf16[64,2304]{1,0:T(8,128)(2,1)S(1)}, bf16[64,2304]{1,0:T(8,128)(2,1)S(1)}, u32[]{:S(2)}, u32[]{:S(2)}) collective-permute-start(bf16[64,2304]{1,0:T(8,128)(2,1)S(1)} %get-tuple-element.164), channel_id=1, source_target_pairs={{0,8},{8,0},{16,24},{24,16},{1,9},{9,1},{17,25},{25,17},{2,10},{10... | collective-permute-start | bytes 884744 | tf_op jit(solution)/shard_map/ppermute | solution.py:101
  521.5 16.3 %collective-permute-start.45 = (f32[64,2304]{1,0:T(8,128)S(1)}, f32[64,2304]{1,0:T(8,128)}, u32[]{:S(2)}, u32[]{:S(2)}) collective-permute-start(f32[64,2304]{1,0:T(8,128)S(1)} %last_grad.1), channel_id=1, source_target_pairs={{0,1},{1,0},{2,3},{3,2},{4,5},{5,4},{6,7},{7,6},{8,9},{9,8},{10,11... | collective-permute-start | bytes 1769480 | tf_op jit(solution)/shard_map/ppermute | solution.py:104
  521.7 65.7 %all-to-all-start.4 = ((bf16[4,144,2304]{2,1,0:T(8,128)(2,1)}), bf16[4,144,2304]{2,1,0:T(8,128)(2,1)}, u32[]{:S(2)}, u32[]{:S(2)}) async-start(bf16[4,144,2304]{2,1,0:T(8,128)(2,1)} %reduce-scatter.8.cloned.1.call-done), calls=%async_computation.7 | async-start | bytes 5308416 | tf_op jit(solution)/shard_map/all_to_all | solution.py:140
  587.4 29.2 %all-to-all-start.5 = ((bf16[4,144,896]{2,1,0:T(8,128)(2,1)}), bf16[4,144,896]{2,1,0:T(8,128)(2,1)S(1)}, u32[]{:S(2)}, u32[]{:S(2)}) async-start(bf16[4,144,896]{2,1,0:T(8,128)(2,1)} %reduce-scatter.6.cloned.1.call-done), calls=%async_computation.8 | async-start | bytes 2064384 | tf_op jit(solution)/shard_map/all_to_all | solution.py:140
  (113 other events, 1019.8 us)
Sparse Core Ops, SparseCore 0:
  23.3 45.9 all-gather.3
Sparse Core Ops, SparseCore 1:
  93.6 64.4 all-gather.5
  161.5 108.1 all-gather.7
  343.2 60.6 reduce-scatter.3
  406.9 112.9 reduce-scatter.7
  523.5 52.0 reduce-scatter.5
